TPU v7x, 256 devices: a whole 4x4x8 slice. The times are simulated.
256 devices in a mesh: replica: 16 (over z_hi, y), fsdp: 16 (over z_lo, x, core).
Axes of the slice: x: 4, y: 4, z: 8 (z_hi: 4, z_lo: 2; z = z_hi * 2 + z_lo), core: 2. Of those that a mesh axis runs over, the one named last changes fastest.
Arguments:
- inner_weights: bfloat16 [16, 4, 1024, 8192], P('replica', None, 'fsdp'), may hold values from -6 to 6
- snapshot: bfloat16 [1024, 8192], P('fsdp'), may hold values from -6 to 6
- momentum: float32 [1024, 8192], P('fsdp', 'replica'), may hold values from -6 to 6
- rand_bits: int32 [16, 1024, 8192], P('replica', 'fsdp'), may hold values from 0 to 4095
- fragment: int32 [1], replicated, may hold values from 0 to 3
Outputs:
- new_snapshot: bfloat16 [1024, 8192], P('fsdp')
- new_momentum: float32 [1024, 8192], P('fsdp', 'replica')
- new_inner: bfloat16 [16, 4, 1024, 8192], P('replica', None, 'fsdp')
Inputs may be any that keep to these rules, and one draw needn't show every extreme that they name: fragment[0] is one of 0, 1, 2, 3, the fragment of the window that syncs.
All inputs are finite; a program needn't handle non-finite values.
Results may differ from a plain program's by a relative error of at most 0.0075.
Values may be sent and summed in bfloat16 or wider, within the bound.
No kernel may reach another device: no remote copies, remote signals or barrier semaphores. Data moves between devices by JAX's collectives and lax.ppermute only.
A program may use at most 64 MiB of HBM per device.

v0:
```python
import jax
import jax.numpy as jnp
from jax import lax
from jax.sharding import PartitionSpec as P

momentum_coef = 0.9
outer_rate = 0.7
blend_keep = 0.5
grid_scale = 4.0
bit_levels = 4096.0


def in_blocks(shard, dim, size):
    dims = shard.shape
    blocks = shard.reshape(*dims[:dim], size, dims[dim] // size, *dims[dim + 1 :])
    return jnp.moveaxis(blocks, dim, 0)


def sent_and_summed(shard, axis, dim):
    blocks = in_blocks(shard, dim, lax.axis_size(axis))
    arrived = lax.all_to_all(blocks, axis, split_axis=0, concat_axis=0, tiled=True)
    return arrived.astype(jnp.float32).sum(axis=0)


def joined_along(blocks, dim):
    dims = list(blocks.shape[1:])
    dims[dim] *= blocks.shape[0]
    return jnp.moveaxis(blocks, 0, dim).reshape(dims)


def sent_to_all(shard, axis):
    size = lax.axis_size(axis)
    return lax.all_to_all(
        jnp.broadcast_to(shard[None], (size, *shard.shape)), axis, 0, 0, tiled=True
    )


def gathered_copies(shard, axis, dim):
    return joined_along(sent_to_all(shard, axis), dim)


def stochastic_grid(snapshot, chosen, rand_bits):
    scaled = grid_scale * (snapshot.astype(jnp.float32) - chosen.astype(jnp.float32))
    lower = jnp.floor(scaled)
    raised = jnp.where(
        rand_bits.astype(jnp.float32) < bit_levels * (scaled - lower), 1.0, 0.0
    ).astype(jnp.float32)
    return ((lower + raised) / grid_scale).astype(jnp.bfloat16)


def outer_update(summed, replicas, momentum, snap_part):
    grad = summed / replicas
    moment_next = momentum_coef * momentum + grad
    snap_next = (
        snap_part.astype(jnp.float32) - outer_rate * (grad + momentum_coef * moment_next)
    ).astype(jnp.bfloat16)
    return (moment_next, snap_next)


def body(inner_weights, snapshot, momentum, rand_bits, fragment):
    fragment_id = fragment[0]
    chosen = lax.dynamic_index_in_dim(inner_weights[0], fragment_id, 0, keepdims=False)
    rounded = stochastic_grid(snapshot, chosen, rand_bits[0]).astype(jnp.float32)
    replicas = lax.axis_size("replica")
    share_cols = momentum.shape[1]
    offset = lax.axis_index("replica") * share_cols
    snap_cols = lax.dynamic_slice_in_dim(snapshot, offset, share_cols, 1)
    summed = sent_and_summed(rounded.astype(jnp.bfloat16), "replica", 1)
    new_momentum, snap_share = outer_update(summed, replicas, momentum, snap_cols)
    new_snapshot = gathered_copies(snap_share, "replica", 1)
    blended = (
        blend_keep * chosen.astype(jnp.float32)
        + (1.0 - blend_keep) * new_snapshot.astype(jnp.float32)
    ).astype(jnp.bfloat16)
    picked = lax.broadcasted_iota(jnp.int32, (1, inner_weights.shape[1], 1, 1), 1) == fragment_id
    new_inner = jnp.where(picked, blended[None, None], inner_weights)
    return (new_snapshot, new_momentum, new_inner)


def solution(mesh):
    placed = (
        P("replica", None, "fsdp", None),
        P("fsdp", None),
        P("fsdp", "replica"),
        P("replica", "fsdp", None),
        P(),
    )
    return jax.shard_map(
        body,
        mesh=mesh,
        in_specs=placed,
        out_specs=(P("fsdp", None), P("fsdp", "replica"), P("replica", None, "fsdp", None)),
        check_vma=False,
    )
```

profile of v0, /device:TPU:2, one launch (start us, length us, event | category | flops | bytes accessed | tf_op | source)
XLA Modules:
  0.0 93.7 jit_solution(16675236293592972424)
XLA Ops:
  1.3 3.0 %fusion.7 = bf16[64,8192]{1,0:T(8,128)(2,1)S(1)} fusion(s32[1,64,8192]{2,1,0:T(8,128)} %param.8, bf16[64,8192]{1,0:T(8,128)(2,1)} %param.6, bf16[1,4,64,8192]{3,2,1,0:T(8,128)(2,1)} %param.5, s32[]{:T(128)S(6)} %select_n.16), kind=kLoop, calls=%fused_computation.12 | loop fusion | flops 6815744 | bytes 5242884 | tf_op jit(solution)/shard_map/convert_element_type | solution.py:48
  4.3 0.4 copy.12
  4.7 1.5 %copy.8 = bf16[16,64,512]{2,1,0:T(8,128)(2,1)} copy(bf16[16,64,512]{2,0,1:T(8,128)(2,1)S(1)} %bitcast.28) | data formatting | bytes 2097152 | tf_op jit(solution)/shard_map/transpose | solution.py:16
  6.2 0.0 copy-start.1
  6.2 11.3 %all-to-all-start = ((bf16[16,64,512]{2,1,0:T(8,128)(2,1)}), bf16[16,64,512]{2,1,0:T(8,128)(2,1)S(1)}, u32[]{:S(2)}, u32[]{:S(2)}) async-start(bf16[16,64,512]{2,1,0:T(8,128)(2,1)} %copy.8), calls=%async_computation | async-start | bytes 2097152 | tf_op jit(solution)/shard_map/all_to_all | solution.py:21
  17.6 28.1 %all-to-all-done = bf16[16,64,512]{2,1,0:T(8,128)(2,1)S(1)} async-done(((bf16[16,64,512]{2,1,0:T(8,128)(2,1)}), bf16[16,64,512]{2,1,0:T(8,128)(2,1)S(1)}, u32[]{:S(2)}, u32[]{:S(2)}) %all-to-all-start) | async-done | bytes 1048608 | tf_op jit(solution)/shard_map/all_to_all | solution.py:21
  45.7 0.1 convert_reduce_fusion
  45.8 0.0 copy-done.1
  45.8 1.5 %subtract_convert_fusion = (bf16[64,512]{1,0:T(8,128)(2,1)S(1)}, f32[64,512]{1,0:T(8,128)}) fusion(f32[64,512]{1,0:T(8,128)S(1)} %convert_reduce_fusion, bf16[64,8192]{1,0:T(8,128)(2,1)} %param.6, s32[]{:T(128)S(6)} %select_n.15, f32[64,512]{1,0:T(8,128)S(1)} %copy-done.1), kind=kLoop, calls=%fused_computation.16 | loop fusion | flops 294912 | bytes 524292 | tf_op jit(solution)/shard_map/convert_element_type | solution.py:56
  47.4 1.1 %broadcast_in_dim.35 = bf16[16,64,512]{2,1,0:T(8,128)(2,1)} broadcast(bf16[64,512]{1,0:T(8,128)(2,1)S(1)} %get-tuple-element.3), dimensions={1,2} | broadcast | bytes 1114112 | tf_op jit(solution)/shard_map/broadcast_in_dim | solution.py:34
  48.4 5.7 %all-to-all-start.1 = ((bf16[16,64,512]{2,1,0:T(8,128)(2,1)}), bf16[16,64,512]{2,1,0:T(8,128)(2,1)S(1)}, u32[]{:S(2)}, u32[]{:S(2)}) async-start(bf16[16,64,512]{2,1,0:T(8,128)(2,1)} %broadcast_in_dim.35), calls=%async_computation.1 | async-start | bytes 2097152 | tf_op jit(solution)/shard_map/all_to_all | solution.py:33
  54.2 28.9 %all-to-all-done.1 = bf16[16,64,512]{2,1,0:T(8,128)(2,1)S(1)} async-done(((bf16[16,64,512]{2,1,0:T(8,128)(2,1)}), bf16[16,64,512]{2,1,0:T(8,128)(2,1)S(1)}, u32[]{:S(2)}, u32[]{:S(2)}) %all-to-all-start.1) | async-done | bytes 1048608 | tf_op jit(solution)/shard_map/all_to_all | solution.py:33
  83.0 1.1 %copy.11 = bf16[16,8,8,512]{3,2,0,1:T(8,128)(2,1)} copy(bf16[16,8,8,512]{3,2,1,0:T(8,128)(2,1)S(1)} %bitcast.27) | data formatting | bytes 2097152 | tf_op jit(solution)/shard_map/reshape | solution.py:28
  84.1 0.3 bitcast_convert_fusion
  84.4 2.5 %copy.10 = f32[64,16,512]{2,1,0:T(8,128)} copy(f32[64,16,512]{2,0,1:T(8,128)S(1)} %bitcast_convert_fusion) | data formatting | bytes 4194304 | tf_op jit(solution)/shard_map/convert_element_type | solution.py:73
  86.9 1.7 %reshape.42 = f32[1,1,64,8192]{3,2,1,0:T(8,128)S(1)} reshape(f32[64,16,512]{2,1,0:T(8,128)} %copy.10) | data formatting | bytes 4194304 | tf_op jit(solution)/shard_map/convert_element_type | solution.py:73
  88.7 0.0 copy-start
  88.7 1.6 %fusion.8 = bf16[64,8192]{1,0:T(8,128)(2,1)S(1)} fusion(f32[1,1,64,8192]{3,2,1,0:T(8,128)S(1)} %reshape.42, bf16[1,4,64,8192]{3,2,1,0:T(8,128)(2,1)} %param.5, s32[]{:T(128)S(6)} %select_n.16), kind=kLoop, calls=%fused_computation.14 | loop fusion | flops 2097152 | bytes 4194308 | tf_op jit(solution)/shard_map/jit(_where)/broadcast_in_dim | solution.py:76
  90.3 0.9 copy-done
  91.2 2.5 %broadcast_select_fusion = bf16[1,4,64,8192]{3,2,1,0:T(8,128)(2,1)} fusion(bf16[1,4,64,8192]{3,2,1,0:T(8,128)(2,1)S(1)} %copy-done, pred[4]{0:T(512)(128)(4,1)S(1)} %iota_compare_fusion, bf16[64,8192]{1,0:T(8,128)(2,1)S(1)} %fusion.8), kind=kLoop, calls=%fused_computation | loop fusion | flops 2097152 | bytes 9437188 | tf_op jit(solution)/shard_map/jit(_where)/select_n | solution.py:76
  (1 shorter events, 0.0 us)
Async XLA Ops:
  6.2 39.6 %copy-start.1 = (f32[64,512]{1,0:T(8,128)S(1)}, f32[64,512]{1,0:T(8,128)}, u32[]{:S(2)}) copy-start(f32[64,512]{1,0:T(8,128)} %param.7) | copy-start | bytes 393220
  6.2 39.4 %all-to-all-start = ((bf16[16,64,512]{2,1,0:T(8,128)(2,1)}), bf16[16,64,512]{2,1,0:T(8,128)(2,1)S(1)}, u32[]{:S(2)}, u32[]{:S(2)}) async-start(bf16[16,64,512]{2,1,0:T(8,128)(2,1)} %copy.8), calls=%async_computation | async-start | bytes 2097152 | tf_op jit(solution)/shard_map/all_to_all | solution.py:21
  48.4 34.6 %all-to-all-start.1 = ((bf16[16,64,512]{2,1,0:T(8,128)(2,1)}), bf16[16,64,512]{2,1,0:T(8,128)(2,1)S(1)}, u32[]{:S(2)}, u32[]{:S(2)}) async-start(bf16[16,64,512]{2,1,0:T(8,128)(2,1)} %broadcast_in_dim.35), calls=%async_computation.1 | async-start | bytes 2097152 | tf_op jit(solution)/shard_map/all_to_all | solution.py:33
  88.7 2.5 %copy-start = (bf16[1,4,64,8192]{3,2,1,0:T(8,128)(2,1)S(1)}, bf16[1,4,64,8192]{3,2,1,0:T(8,128)(2,1)}, u32[]{:S(2)}) copy-start(bf16[1,4,64,8192]{3,2,1,0:T(8,128)(2,1)} %param.5) | copy-start | bytes 12582916
where the time goes:
time: 94 us; the launch traced here: 93.7 us
  waiting for transfers between devices  57 us (61%)
  starting transfers between devices  17.1 us (18%)
  local copies, waits for them, and re-layouts  9.19 us (10%)
  other arithmetic  9.13 us (10%)
  between operations  1.36 us (1%)
    all_to_all x1, waiting for transfers between devices, sent_to_all(): lax.all_to_all(jnp.broadcast_to(shard[None], (size, *shard.shape)), axis,...  28.9 us
    all_to_all x1, waiting for transfers between devices, sent_and_summed(): lax.all_to_all(blocks, axis, split_axis=0, concat_axis=0, tiled=True)  28.1 us
    all_to_all x1, starting transfers between devices, sent_and_summed(): lax.all_to_all(blocks, axis, split_axis=0, concat_axis=0, tiled=True)  11.3 us
    all_to_all x1, starting transfers between devices, sent_to_all(): lax.all_to_all(jnp.broadcast_to(shard[None], (size, *shard.shape)), axis,...  5.72 us
    convert_element_type x2, local copies, waits for them, and re-layouts, body(): new_snapshot.astype(jnp.float32)  4.29 us
    convert_element_type x1, other arithmetic, stochastic_grid(): return ((lower + raised) / grid_scale).astype(jnp.bfloat16)  3.03 us
    select_n x1, other arithmetic, body(): new_inner = jnp.where(picked, blended[None, None], inner_weights)  2.51 us
  transfers between devices with their start and end apart: 2, of which 2 were waited for; matrix products, arithmetic and copies ran while one was open for 0% of the time, Pallas kernels for 0%

commit v1 on v0

v1 whole, which is shorter than its diff:
```python
import functools

import jax
import jax.numpy as jnp
from jax import lax
from jax.experimental import pallas as pl
from jax.experimental.pallas import tpu as pltpu
from jax.sharding import PartitionSpec as P

momentum_coef = 0.9
outer_rate = 0.7
blend_keep = 0.5
grid_scale = 4.0
bit_levels = 4096.0

Y = 4
Z = 4
CHUNKS = 2
ROWS = 32


def y_shift(k):
    return [(z * Y + y, z * Y + (y + k) % Y) for z in range(Z) for y in range(Y)]


def z_swap(s):
    return [(z * Y + y, (z ^ s) * Y + y) for z in range(Z) for y in range(Y)]


def round_kernel(share, ids, inner_ref, snap_ref, bits_ref, *outs):
    for k in range(Y):
        cols = pl.ds(pl.multiple_of(lax.rem(ids[1] + k, Y) * share, share), share)
        snap = snap_ref[:, cols].astype(jnp.float32)
        scaled = grid_scale * (snap - inner_ref[0, 0, :, cols].astype(jnp.float32))
        lower = jnp.floor(scaled)
        raised = jnp.where(
            bits_ref[0, :, cols].astype(jnp.float32) < bit_levels * (scaled - lower), 1.0, 0.0
        )
        centred = lower - jnp.floor(grid_scale * snap) + raised
        outs[k][...] = centred.astype(jnp.bfloat16)


def rounded_blocks(ids, inner, snapshot, bits, chunk, share):
    rows = snapshot.shape[0]
    wide = Y * share
    per = Z // CHUNKS
    first = chunk * per
    return pl.pallas_call(
        functools.partial(round_kernel, share),
        out_shape=[jax.ShapeDtypeStruct((rows, per * share), jnp.bfloat16)] * Y,
        grid_spec=pltpu.PrefetchScalarGridSpec(
            num_scalar_prefetch=1,
            grid=(per, rows // ROWS),
            in_specs=[
                pl.BlockSpec((1, 1, ROWS, wide), lambda j, i, ids: (0, ids[0], i, first + j)),
                pl.BlockSpec((ROWS, wide), lambda j, i, ids: (i, first + j)),
                pl.BlockSpec((1, ROWS, wide), lambda j, i, ids: (0, i, first + j)),
            ],
            out_specs=[pl.BlockSpec((ROWS, share), lambda j, i, ids: (i, j))] * Y,
        ),
        compiler_params=pltpu.CompilerParams(vmem_limit_bytes=8 << 20),
        cost_estimate=pl.CostEstimate(
            flops=12 * rows * per * wide, bytes_accessed=10 * rows * per * wide, transcendentals=0
        ),
        name=f"round{chunk}",
    )(ids, inner, snapshot, bits)


def copy_kernel(ids, inner_ref, out_ref, sems):
    frags = inner_ref.shape[1]
    copies = []
    for n in range(1, frags):
        f = lax.rem(ids[0] + n, frags)
        copies.append(pltpu.make_async_copy(inner_ref.at[0, f], out_ref.at[0, f], sems.at[n - 1]))
    for c in copies:
        c.start()
    for c in copies:
        c.wait()


def others_copied(ids, inner):
    frags = inner.shape[1]
    return pl.pallas_call(
        copy_kernel,
        out_shape=jax.ShapeDtypeStruct(inner.shape, inner.dtype),
        grid_spec=pltpu.PrefetchScalarGridSpec(
            num_scalar_prefetch=1,
            grid=(),
            in_specs=[pl.BlockSpec(memory_space=pl.ANY)],
            out_specs=pl.BlockSpec(memory_space=pl.ANY),
            scratch_shapes=[pltpu.SemaphoreType.DMA((frags - 1,))],
        ),
        compiler_params=pltpu.CompilerParams(vmem_limit_bytes=1 << 20),
        cost_estimate=pl.CostEstimate(flops=0, bytes_accessed=3 * inner.size, transcendentals=0),
        name="others",
    )(ids, inner)


def blend_kernel(share, ids, inner_ref, *refs):
    blocks, (snap_out, inner_out) = refs[:Y], refs[-2:]
    for k in range(Y):
        cols = pl.ds(pl.multiple_of(lax.rem(ids[1] + Y - k, Y) * share, share), share)
        new = blocks[k][...]
        snap_out[:, cols] = new
        inner_out[0, 0, :, cols] = (
            blend_keep * inner_ref[0, 0, :, cols].astype(jnp.float32)
            + (1.0 - blend_keep) * new.astype(jnp.float32)
        ).astype(jnp.bfloat16)


def blended(ids, inner, blocks, snap_out, inner_out, chunk, share):
    rows = blocks[0].shape[0]
    wide = Y * share
    per = Z // CHUNKS
    first = chunk * per
    inner_spec = pl.BlockSpec((1, 1, ROWS, wide), lambda j, i, ids: (0, ids[0], i, first + j))
    snap_spec = pl.BlockSpec((ROWS, wide), lambda j, i, ids: (i, first + j))
    kept = [inner_out] if snap_out is None else [snap_out, inner_out]
    last = 1 + 1 + Y + len(kept) - 1
    aliases = {last: 1} if snap_out is None else {last - 1: 0, last: 1}
    return pl.pallas_call(
        functools.partial(blend_kernel, share),
        out_shape=[
            jax.ShapeDtypeStruct((rows, Z * wide), jnp.bfloat16),
            jax.ShapeDtypeStruct(inner.shape, inner.dtype),
        ],
        grid_spec=pltpu.PrefetchScalarGridSpec(
            num_scalar_prefetch=1,
            grid=(per, rows // ROWS),
            in_specs=[inner_spec]
            + [pl.BlockSpec((ROWS, share), lambda j, i, ids: (i, j))] * Y
            + [pl.BlockSpec(memory_space=pl.ANY)] * len(kept),
            out_specs=[snap_spec, inner_spec],
        ),
        input_output_aliases=aliases,
        compiler_params=pltpu.CompilerParams(vmem_limit_bytes=8 << 20),
        cost_estimate=pl.CostEstimate(
            flops=4 * rows * per * wide, bytes_accessed=8 * rows * per * wide, transcendentals=0
        ),
        name=f"blend{chunk}",
    )(ids, inner, *blocks, *kept)


def body(inner, snapshot, momentum, bits, fragment):
    f32 = jnp.float32
    share = momentum.shape[1]
    me = lax.axis_index("replica")
    y, z = me % Y, me // Y
    ids = jnp.stack([fragment[0], y.astype(jnp.int32)])
    per = Z // CHUNKS

    near = lax.ppermute(momentum, "replica", z_swap(1))
    odd = z % 2 == 1
    mine = jnp.concatenate(
        [jnp.where(odd, near, momentum), jnp.where(odd, momentum, near)], axis=1
    )
    far = lax.ppermute(mine, "replica", z_swap(3))
    high = z // 2 == 1
    moments = jnp.concatenate([jnp.where(high, far, mine), jnp.where(high, mine, far)], axis=1)
    snaps = jnp.concatenate(
        [lax.dynamic_slice_in_dim(snapshot, (b * Y + y) * share, share, 1) for b in range(Z)], axis=1
    )

    sent = [rounded_blocks(ids, inner, snapshot, bits, c, share) for c in range(CHUNKS)]
    others = others_copied(ids, inner)
    totals, news = [], []
    for c in range(CHUNKS):
        got = [sent[c][0]] + [lax.ppermute(sent[c][k], "replica", y_shift(k)) for k in range(1, Y)]
        part = sum(g.astype(f32) for g in got).astype(jnp.bfloat16)
        order = (1, 3) if c % 2 == 0 else (3, 1)
        part = (
            part.astype(f32) + lax.ppermute(part, "replica", z_swap(order[0])).astype(f32)
        ).astype(jnp.bfloat16)
        total = part.astype(f32) + lax.ppermute(part, "replica", z_swap(order[1])).astype(f32)
        at = slice(c * per * share, (c + 1) * per * share)
        snap = snaps[:, at].astype(f32)
        grad = (total + (Y * Z) * jnp.floor(grid_scale * snap)) / (grid_scale * Y * Z)
        moment = momentum_coef * moments[:, at] + grad
        totals.append(grad)
        news.append((snap - outer_rate * (grad + momentum_coef * moment)).astype(jnp.bfloat16))

    snap_out, inner_out = None, others
    for c in range(CHUNKS):
        blocks = [news[c]] + [lax.ppermute(news[c], "replica", y_shift(k)) for k in range(1, Y)]
        snap_out, inner_out = blended(ids, inner, blocks, snap_out, inner_out, c, share)

    grads = jnp.concatenate(totals, axis=1)
    own = grads[:, :share]
    for b in range(1, Z):
        own = jnp.where(z == b, grads[:, b * share : (b + 1) * share], own)
    return snap_out, momentum_coef * momentum + own, inner_out


def solution(mesh):
    placed = (
        P("replica", None, "fsdp", None),
        P("fsdp", None),
        P("fsdp", "replica"),
        P("replica", "fsdp", None),
        P(),
    )
    return jax.shard_map(
        body,
        mesh=mesh,
        in_specs=placed,
        out_specs=(P("fsdp", None), P("fsdp", "replica"), P("replica", None, "fsdp", None)),
        check_vma=False,
    )
```

time: 94 us -> 74.8 us (0.80)
  waiting for transfers between devices: 57 us -> 21.9 us
  starting transfers between devices: 17.1 us -> 32 us
  Pallas kernels: 0 us -> 9.66 us
  other arithmetic: 9.13 us -> 1.33 us
  local copies, waits for them, and re-layouts: 9.19 us -> 8.15 us
    all_to_all x2 -> x0, waiting for transfers between devices: 57 us -> none  [the longest x1 28.9 us: sent_to_all(): lax.all_to_all(jnp.broadcast_to(shard[None], (size, *shard.shape)), axis,...]
    ppermute x0 -> x18, starting transfers between devices: none -> 32 us  [the longest x6 9.55 us: body(): lax.ppermute(sent[c][k], 'replica', y_shift(k))]
    ppermute x0 -> x18, waiting for transfers between devices: none -> 21.9 us  [the longest x2 13.6 us: body(): lax.ppermute(part, 'replica', z_swap(order[0])).astype(f32)]
    all_to_all x2 -> x0, starting transfers between devices: 17.1 us -> none  [the longest x1 11.3 us: sent_and_summed(): lax.all_to_all(blocks, axis, split_axis=0, concat_axis=0, tiled=True)]
    pallas_call x0 -> x5, Pallas kernels: none -> 9.66 us  [the longest x2 4.5 us: blended(): pl.pallas_call(functools.partial(blend_kernel, share), out_shape=[jax.Sha...]
    unnamed x5 -> x12, local copies, waits for them, and re-layouts: 1.21 us -> 7.2 us
    convert_element_type x3 -> x5, other arithmetic: 4.84 us -> 0.51 us  [the longest x1 0.29 us: body(): (snap - outer_rate * (grad + momentum_coef * moment)).astype(jnp.bfloat16)]
    convert_element_type x2 -> x0, local copies, waits for them, and re-layouts: 4.29 us -> none  [body(): new_snapshot.astype(jnp.float32)]
  transfers between devices with their start and end apart: 2 -> 18, of which waited for: 2 -> 8; matrix products, arithmetic and copies ran while one was open for 0% -> 3% of each run, Pallas kernels for 0% -> 10%
where the time goes in v1:
time: 74.8 us; the launch traced here: 74.5 us
  starting transfers between devices  32 us (43%)
  waiting for transfers between devices  21.9 us (29%)
  Pallas kernels  9.66 us (13%)
  local copies, waits for them, and re-layouts  8.15 us (11%)
  between operations  1.41 us (2%)
  other arithmetic  1.33 us (2%)
    ppermute x2, waiting for transfers between devices, body(): lax.ppermute(part, 'replica', z_swap(order[0])).astype(f32)  13.6 us
    ppermute x6, starting transfers between devices, body(): lax.ppermute(sent[c][k], 'replica', y_shift(k))  9.55 us
    ppermute x6, starting transfers between devices, body(): lax.ppermute(news[c], 'replica', y_shift(k))  7.75 us
    unnamed x12, local copies, waits for them, and re-layouts  7.2 us
    ppermute x2, starting transfers between devices, body(): lax.ppermute(part, 'replica', z_swap(order[0])).astype(f32)  4.72 us
    pallas_call x2, Pallas kernels, blended(): pl.pallas_call(functools.partial(blend_kernel, share), out_shape=[jax.Sha...  4.5 us
    ppermute x1, starting transfers between devices, body(): far = lax.ppermute(mine, 'replica', z_swap(3))  4.48 us
    ppermute x2, waiting for transfers between devices, body(): lax.ppermute(part, 'replica', z_swap(order[1])).astype(f32)  4.34 us
  transfers between devices with their start and end apart: 18, of which 8 were waited for; matrix products, arithmetic and copies ran while one was open for 3% of the time, Pallas kernels for 10%

profile of v1, /device:TPU:2, one launch (start us, length us, event | category | flops | bytes accessed | tf_op | source)
XLA Modules:
  0.0 74.5 jit_solution(11723811461712708153)
XLA Ops:
  0.6 3.4 %collective-permute-start.5 = (f32[64,512]{1,0:T(8,128)}, f32[64,512]{1,0:T(8,128)S(1)}, u32[]{:S(2)}, u32[]{:S(2)}) collective-permute-start(f32[64,512]{1,0:T(8,128)} %param.7), channel_id=1, source_target_pairs={{0,64},{16,80},{32,96},{48,112},{64,0},{80,16},{96,32},{112,48},{1... | collective-permute-start | bytes 393224 | tf_op jit(solution)/shard_map/ppermute | solution.py:152
  4.7 2.2 %copy-done = bf16[1,4,64,8192]{3,2,1,0:T(8,128)(2,1)S(1)} copy-done((bf16[1,4,64,8192]{3,2,1,0:T(8,128)(2,1)S(1)}, bf16[1,4,64,8192]{3,2,1,0:T(8,128)(2,1)}, u32[]{:S(2)}) %copy-start) | copy-done | bytes 4194328
  6.9 1.6 %copy-done.3 = s32[1,64,8192]{2,1,0:T(8,128)S(1)} copy-done((s32[1,64,8192]{2,1,0:T(8,128)S(1)}, s32[1,64,8192]{2,1,0:T(8,128)}, u32[]{:S(2)}) %copy-start.3) | copy-done | bytes 2097176
  9.7 1.5 %round0.1 = (bf16[64,1024]{1,0:T(8,128)(2,1)S(1)}, bf16[64,1024]{1,0:T(8,128)(2,1)S(1)}, bf16[64,1024]{1,0:T(8,128)(2,1)S(1)}, bf16[64,1024]{1,0:T(8,128)(2,1)S(1)}) custom-call(s32[2]{0:T(128)S(1)} %pad_add_fusion.ids, bf16[1,4,64,8192]{3,2,1,0:T(8,128)(2,1)S(1)} %copy-done, bf16[64,8192]{1,0:T(8,128)(2,1)S(1)} %copy-done.4, s32[1,64,8192]{2,1,0:T(8,128)S(1)} %copy-done.3), custom_call_target="tpu_custom_call" | custom-call | flops 3145728 | bytes 2621440 | tf_op jit(solution)/shard_map/round0/pallas_call | solution.py:48
  11.2 1.7 %collective-permute-start.10 = (bf16[64,1024]{1,0:T(8,128)(2,1)S(1)}, bf16[64,1024]{1,0:T(8,128)(2,1)S(1)}, u32[]{:S(2)}, u32[]{:S(2)}) collective-permute-start(bf16[64,1024]{1,0:T(8,128)(2,1)S(1)} %get-tuple-element.20), channel_id=1, source_target_pairs={{0,16},{16,32},{32,48},{48,0},{64,80},{80,96},{96,112},{112,64},{1... | collective-permute-start | bytes 393224 | tf_op jit(solution)/shard_map/ppermute | solution.py:168
  12.8 2.9 %collective-permute-start.11 = (bf16[64,1024]{1,0:T(8,128)(2,1)S(1)}, bf16[64,1024]{1,0:T(8,128)(2,1)S(1)}, u32[]{:S(2)}, u32[]{:S(2)}) collective-permute-start(bf16[64,1024]{1,0:T(8,128)(2,1)S(1)} %get-tuple-element.21), channel_id=1, source_target_pairs={{0,32},{16,48},{32,0},{48,16},{64,96},{80,112},{96,64},{112,80},{1... | collective-permute-start | bytes 393224 | tf_op jit(solution)/shard_map/ppermute | solution.py:168
  15.8 1.3 %collective-permute-start.12 = (bf16[64,1024]{1,0:T(8,128)(2,1)S(1)}, bf16[64,1024]{1,0:T(8,128)(2,1)S(1)}, u32[]{:S(2)}, u32[]{:S(2)}) collective-permute-start(bf16[64,1024]{1,0:T(8,128)(2,1)S(1)} %get-tuple-element.22), channel_id=1, source_target_pairs={{0,48},{16,0},{32,16},{48,32},{64,112},{80,64},{96,80},{112,96},{1... | collective-permute-start | bytes 393224 | tf_op jit(solution)/shard_map/ppermute | solution.py:168
  17.1 1.5 %round1.1 = (bf16[64,1024]{1,0:T(8,128)(2,1)S(1)}, bf16[64,1024]{1,0:T(8,128)(2,1)S(1)}, bf16[64,1024]{1,0:T(8,128)(2,1)S(1)}, bf16[64,1024]{1,0:T(8,128)(2,1)S(1)}) custom-call(s32[2]{0:T(128)S(1)} %pad_add_fusion.ids, bf16[1,4,64,8192]{3,2,1,0:T(8,128)(2,1)S(1)} %copy-done, bf16[64,8192]{1,0:T(8,128)(2,1)S(1)} %copy-done.4, s32[1,64,8192]{2,1,0:T(8,128)S(1)} %copy-done.3), custom_call_target="tpu_custom_call" | custom-call | flops 3145728 | bytes 2621440 | tf_op jit(solution)/shard_map/round1/pallas_call | solution.py:48
  20.2 2.1 %collective-permute-start.2 = (bf16[64,1024]{1,0:T(8,128)(2,1)S(1)}, bf16[64,1024]{1,0:T(8,128)(2,1)S(1)}, u32[]{:S(2)}, u32[]{:S(2)}) collective-permute-start(bf16[64,1024]{1,0:T(8,128)(2,1)S(1)} %get-tuple-element.18), channel_id=1, source_target_pairs={{0,48},{16,0},{32,16},{48,32},{64,112},{80,64},{96,80},{112,96},{1... | collective-permute-start | bytes 393224 | tf_op jit(solution)/shard_map/ppermute | solution.py:168
  23.0 4.5 %collective-permute-start.6 = (f32[64,1024]{1,0:T(8,128)S(1)}, f32[64,1024]{1,0:T(8,128)S(1)}, u32[]{:S(2)}, u32[]{:S(2)}) collective-permute-start(f32[64,1024]{1,0:T(8,128)S(1)} %pad_maximum_fusion), channel_id=1, source_target_pairs={{0,192},{16,208},{32,224},{48,240},{64,128},{80,144},{96,160},{112... | collective-permute-start | bytes 786440 | tf_op jit(solution)/shard_map/ppermute | solution.py:157
  27.5 1.6 %collective-permute-start.13 = (bf16[64,1024]{1,0:T(8,128)(2,1)S(1)}, bf16[64,1024]{1,0:T(8,128)(2,1)S(1)}, u32[]{:S(2)}, u32[]{:S(2)}) collective-permute-start(bf16[64,1024]{1,0:T(8,128)(2,1)S(1)} %add_convert_fusion.1), channel_id=1, source_target_pairs={{0,64},{16,80},{32,96},{48,112},{64,0},{80,16},{96,32},{112,48},{1... | collective-permute-start | bytes 393224 | tf_op jit(solution)/shard_map/ppermute | solution.py:172
  29.2 3.2 %collective-permute-start.3 = (bf16[64,1024]{1,0:T(8,128)(2,1)S(1)}, bf16[64,1024]{1,0:T(8,128)(2,1)S(1)}, u32[]{:S(2)}, u32[]{:S(2)}) collective-permute-start(bf16[64,1024]{1,0:T(8,128)(2,1)S(1)} %add_convert_fusion.3), channel_id=1, source_target_pairs={{0,192},{16,208},{32,224},{48,240},{64,128},{80,144},{96,160},{112... | collective-permute-start | bytes 393224 | tf_op jit(solution)/shard_map/ppermute | solution.py:172
  32.3 1.8 %collective-permute-done.13 = bf16[64,1024]{1,0:T(8,128)(2,1)S(1)} collective-permute-done((bf16[64,1024]{1,0:T(8,128)(2,1)S(1)}, bf16[64,1024]{1,0:T(8,128)(2,1)S(1)}, u32[]{:S(2)}, u32[]{:S(2)}) %collective-permute-start.13) | collective-permute-done | bytes 131104 | tf_op jit(solution)/shard_map/ppermute | solution.py:172
  34.3 11.8 %collective-permute-done.3 = bf16[64,1024]{1,0:T(8,128)(2,1)S(1)} collective-permute-done((bf16[64,1024]{1,0:T(8,128)(2,1)S(1)}, bf16[64,1024]{1,0:T(8,128)(2,1)S(1)}, u32[]{:S(2)}, u32[]{:S(2)}) %collective-permute-start.3) | collective-permute-done | bytes 131104 | tf_op jit(solution)/shard_map/ppermute | solution.py:172
  46.1 2.1 %collective-permute-start.4 = (bf16[64,1024]{1,0:T(8,128)(2,1)S(1)}, bf16[64,1024]{1,0:T(8,128)(2,1)S(1)}, u32[]{:S(2)}, u32[]{:S(2)}) collective-permute-start(bf16[64,1024]{1,0:T(8,128)(2,1)S(1)} %add_convert_fusion.2), channel_id=1, source_target_pairs={{0,64},{16,80},{32,96},{48,112},{64,0},{80,16},{96,32},{112,48},{1... | collective-permute-start | bytes 393224 | tf_op jit(solution)/shard_map/ppermute | solution.py:174
  49.1 4.3 %collective-permute-done.4 = bf16[64,1024]{1,0:T(8,128)(2,1)S(1)} collective-permute-done((bf16[64,1024]{1,0:T(8,128)(2,1)S(1)}, bf16[64,1024]{1,0:T(8,128)(2,1)S(1)}, u32[]{:S(2)}, u32[]{:S(2)}) %collective-permute-start.4) | collective-permute-done | bytes 131104 | tf_op jit(solution)/shard_map/ppermute | solution.py:174
  53.8 1.4 %collective-permute-start.17 = (bf16[64,1024]{1,0:T(8,128)(2,1)S(1)}, bf16[64,1024]{1,0:T(8,128)(2,1)S(1)}, u32[]{:S(2)}, u32[]{:S(2)}) collective-permute-start(bf16[64,1024]{1,0:T(8,128)(2,1)S(1)} %get-tuple-element.31.refs_0_), channel_id=1, source_target_pairs={{0,48},{16,0},{32,16},{48,32},{64,112},{80,64},{96,80},{112,96},{1... | collective-permute-start | bytes 393224 | tf_op jit(solution)/shard_map/ppermute | solution.py:184
  55.2 2.2 %copy-done.1 = bf16[1,4,64,8192]{3,2,1,0:T(8,128)(2,1)S(1)} copy-done((bf16[1,4,64,8192]{3,2,1,0:T(8,128)(2,1)S(1)}, bf16[1,4,64,8192]{3,2,1,0:T(8,128)(2,1)}, u32[]{:S(2)}) %copy-start.1) | copy-done | bytes 4194328
  57.4 2.2 %others.1.refs_4_ = bf16[1,4,64,8192]{3,2,1,0:T(8,128)(2,1)} custom-call(s32[2]{0:T(128)S(1)} %pad_add_fusion.ids, bf16[1,4,64,8192]{3,2,1,0:T(8,128)(2,1)S(1)} %copy-done.1), custom_call_target="tpu_custom_call" | custom-call | bytes 6291456 | tf_op jit(solution)/shard_map/others/pallas_call | solution.py:83
  59.7 1.4 %collective-permute-start.16 = (bf16[64,1024]{1,0:T(8,128)(2,1)S(1)}, bf16[64,1024]{1,0:T(8,128)(2,1)S(1)}, u32[]{:S(2)}, u32[]{:S(2)}) collective-permute-start(bf16[64,1024]{1,0:T(8,128)(2,1)S(1)} %get-tuple-element.31.refs_0_), channel_id=1, source_target_pairs={{0,32},{16,48},{32,0},{48,16},{64,96},{80,112},{96,64},{112,80},{1... | collective-permute-start | bytes 393224 | tf_op jit(solution)/shard_map/ppermute | solution.py:184
  62.3 2.1 %collective-permute-start.9 = (bf16[64,1024]{1,0:T(8,128)(2,1)S(1)}, bf16[64,1024]{1,0:T(8,128)(2,1)S(1)}, u32[]{:S(2)}, u32[]{:S(2)}) collective-permute-start(bf16[64,1024]{1,0:T(8,128)(2,1)S(1)} %get-tuple-element.32.refs_0_), channel_id=1, source_target_pairs={{0,48},{16,0},{32,16},{48,32},{64,112},{80,64},{96,80},{112,96},{1... | collective-permute-start | bytes 393224 | tf_op jit(solution)/shard_map/ppermute | solution.py:184
  66.8 1.3 %collective-permute-done.15.refs_1_ = bf16[64,1024]{1,0:T(8,128)(2,1)S(1)} collective-permute-done((bf16[64,1024]{1,0:T(8,128)(2,1)S(1)}, bf16[64,1024]{1,0:T(8,128)(2,1)S(1)}, u32[]{:S(2)}, u32[]{:S(2)}) %collective-permute-start.15) | collective-permute-done | bytes 131104 | tf_op jit(solution)/shard_map/ppermute | solution.py:184
  68.2 2.2 %blend0.1 = (bf16[64,8192]{1,0:T(8,128)(2,1)}, bf16[1,4,64,8192]{3,2,1,0:T(8,128)(2,1)}) custom-call(s32[2]{0:T(128)S(1)} %pad_add_fusion.ids, bf16[1,4,64,8192]{3,2,1,0:T(8,128)(2,1)S(1)} %copy-done.2, bf16[64,1024]{1,0:T(8,128)(2,1)S(1)} %get-tuple-element.31.refs_0_, ...), custom_call_target="tpu_custom_call", output_to_operand_aliasing={{1}: (6, {})} | custom-call | flops 1048576 | bytes 2097152 | tf_op jit(solution)/shard_map/blend0/pallas_call | solution.py:121
  72.2 2.3 %blend1.1 = (bf16[64,8192]{1,0:T(8,128)(2,1)}, bf16[1,4,64,8192]{3,2,1,0:T(8,128)(2,1)}) custom-call(s32[2]{0:T(128)S(1)} %pad_add_fusion.ids, bf16[1,4,64,8192]{3,2,1,0:T(8,128)(2,1)S(1)} %copy-done.2, bf16[64,1024]{1,0:T(8,128)(2,1)S(1)} %get-tuple-element.32.refs_0_, ...), custom_call_target="tpu_custom_call", output_to_operand_aliasing={{0}: (6, {}), {1}: (7, {})} | custom-call | flops 1048576 | bytes 2097152 | tf_op jit(solution)/shard_map/blend1/pallas_call | solution.py:121
  (39 shorter events, 10.6 us)
Async XLA Ops:
  0.6 18.7 %collective-permute-start.5 = (f32[64,512]{1,0:T(8,128)}, f32[64,512]{1,0:T(8,128)S(1)}, u32[]{:S(2)}, u32[]{:S(2)}) collective-permute-start(f32[64,512]{1,0:T(8,128)} %param.7), channel_id=1, source_target_pairs={{0,64},{16,80},{32,96},{48,112},{64,0},{80,16},{96,32},{112,48},{1... | collective-permute-start | bytes 393224 | tf_op jit(solution)/shard_map/ppermute | solution.py:152
  4.7 2.2 %copy-start = (bf16[1,4,64,8192]{3,2,1,0:T(8,128)(2,1)S(1)}, bf16[1,4,64,8192]{3,2,1,0:T(8,128)(2,1)}, u32[]{:S(2)}) copy-start(bf16[1,4,64,8192]{3,2,1,0:T(8,128)(2,1)} %inner_ref.9) | copy-start | bytes 12582916
  6.9 1.6 %copy-start.3 = (s32[1,64,8192]{2,1,0:T(8,128)S(1)}, s32[1,64,8192]{2,1,0:T(8,128)}, u32[]{:S(2)}) copy-start(s32[1,64,8192]{2,1,0:T(8,128)} %bits_ref.3) | copy-start | bytes 6291460
  8.5 1.2 %copy-start.4 = (bf16[64,8192]{1,0:T(8,128)(2,1)S(1)}, bf16[64,8192]{1,0:T(8,128)(2,1)}, u32[]{:S(2)}) copy-start(bf16[64,8192]{1,0:T(8,128)(2,1)} %snap_ref.3) | copy-start | bytes 3145732
  11.2 9.0 %copy-start.5 = (f32[64,512]{1,0:T(8,128)S(1)}, f32[64,512]{1,0:T(8,128)}, u32[]{:S(2)}) copy-start(f32[64,512]{1,0:T(8,128)} %param.7) | copy-start | bytes 393220
  11.2 9.0 %collective-permute-start.10 = (bf16[64,1024]{1,0:T(8,128)(2,1)S(1)}, bf16[64,1024]{1,0:T(8,128)(2,1)S(1)}, u32[]{:S(2)}, u32[]{:S(2)}) collective-permute-start(bf16[64,1024]{1,0:T(8,128)(2,1)S(1)} %get-tuple-element.20), channel_id=1, source_target_pairs={{0,16},{16,32},{32,48},{48,0},{64,80},{80,96},{96,112},{112,64},{1... | collective-permute-start | bytes 393224 | tf_op jit(solution)/shard_map/ppermute | solution.py:168
  12.8 10.1 %collective-permute-start.11 = (bf16[64,1024]{1,0:T(8,128)(2,1)S(1)}, bf16[64,1024]{1,0:T(8,128)(2,1)S(1)}, u32[]{:S(2)}, u32[]{:S(2)}) collective-permute-start(bf16[64,1024]{1,0:T(8,128)(2,1)S(1)} %get-tuple-element.21), channel_id=1, source_target_pairs={{0,32},{16,48},{32,0},{48,16},{64,96},{80,112},{96,64},{112,80},{1... | collective-permute-start | bytes 393224 | tf_op jit(solution)/shard_map/ppermute | solution.py:168
  15.8 11.7 %collective-permute-start.12 = (bf16[64,1024]{1,0:T(8,128)(2,1)S(1)}, bf16[64,1024]{1,0:T(8,128)(2,1)S(1)}, u32[]{:S(2)}, u32[]{:S(2)}) collective-permute-start(bf16[64,1024]{1,0:T(8,128)(2,1)S(1)} %get-tuple-element.22), channel_id=1, source_target_pairs={{0,48},{16,0},{32,16},{48,32},{64,112},{80,64},{96,80},{112,96},{1... | collective-permute-start | bytes 393224 | tf_op jit(solution)/shard_map/ppermute | solution.py:168
  18.6 10.5 %collective-permute-start = (bf16[64,1024]{1,0:T(8,128)(2,1)S(1)}, bf16[64,1024]{1,0:T(8,128)(2,1)S(1)}, u32[]{:S(2)}, u32[]{:S(2)}) collective-permute-start(bf16[64,1024]{1,0:T(8,128)(2,1)S(1)} %get-tuple-element.16), channel_id=1, source_target_pairs={{0,16},{16,32},{32,48},{48,0},{64,80},{80,96},{96,112},{112,64},{1... | collective-permute-start | bytes 393224 | tf_op jit(solution)/shard_map/ppermute | solution.py:168
  19.3 9.8 %collective-permute-start.1 = (bf16[64,1024]{1,0:T(8,128)(2,1)S(1)}, bf16[64,1024]{1,0:T(8,128)(2,1)S(1)}, u32[]{:S(2)}, u32[]{:S(2)}) collective-permute-start(bf16[64,1024]{1,0:T(8,128)(2,1)S(1)} %get-tuple-element.17), channel_id=1, source_target_pairs={{0,32},{16,48},{32,0},{48,16},{64,96},{80,112},{96,64},{112,80},{1... | collective-permute-start | bytes 393224 | tf_op jit(solution)/shard_map/ppermute | solution.py:168
  20.2 8.9 %collective-permute-start.2 = (bf16[64,1024]{1,0:T(8,128)(2,1)S(1)}, bf16[64,1024]{1,0:T(8,128)(2,1)S(1)}, u32[]{:S(2)}, u32[]{:S(2)}) collective-permute-start(bf16[64,1024]{1,0:T(8,128)(2,1)S(1)} %get-tuple-element.18), channel_id=1, source_target_pairs={{0,48},{16,0},{32,16},{48,32},{64,112},{80,64},{96,80},{112,96},{1... | collective-permute-start | bytes 393224 | tf_op jit(solution)/shard_map/ppermute | solution.py:168
  23.0 26.2 %collective-permute-start.6 = (f32[64,1024]{1,0:T(8,128)S(1)}, f32[64,1024]{1,0:T(8,128)S(1)}, u32[]{:S(2)}, u32[]{:S(2)}) collective-permute-start(f32[64,1024]{1,0:T(8,128)S(1)} %pad_maximum_fusion), channel_id=1, source_target_pairs={{0,192},{16,208},{32,224},{48,240},{64,128},{80,144},{96,160},{112... | collective-permute-start | bytes 786440 | tf_op jit(solution)/shard_map/ppermute | solution.py:157
  27.5 6.6 %collective-permute-start.13 = (bf16[64,1024]{1,0:T(8,128)(2,1)S(1)}, bf16[64,1024]{1,0:T(8,128)(2,1)S(1)}, u32[]{:S(2)}, u32[]{:S(2)}) collective-permute-start(bf16[64,1024]{1,0:T(8,128)(2,1)S(1)} %add_convert_fusion.1), channel_id=1, source_target_pairs={{0,64},{16,80},{32,96},{48,112},{64,0},{80,16},{96,32},{112,48},{1... | collective-permute-start | bytes 393224 | tf_op jit(solution)/shard_map/ppermute | solution.py:172
  29.2 16.9 %collective-permute-start.3 = (bf16[64,1024]{1,0:T(8,128)(2,1)S(1)}, bf16[64,1024]{1,0:T(8,128)(2,1)S(1)}, u32[]{:S(2)}, u32[]{:S(2)}) collective-permute-start(bf16[64,1024]{1,0:T(8,128)(2,1)S(1)} %add_convert_fusion.3), channel_id=1, source_target_pairs={{0,192},{16,208},{32,224},{48,240},{64,128},{80,144},{96,160},{112... | collective-permute-start | bytes 393224 | tf_op jit(solution)/shard_map/ppermute | solution.py:172
  34.2 14.9 %collective-permute-start.14 = (bf16[64,1024]{1,0:T(8,128)(2,1)S(1)}, bf16[64,1024]{1,0:T(8,128)(2,1)S(1)}, u32[]{:S(2)}, u32[]{:S(2)}) collective-permute-start(bf16[64,1024]{1,0:T(8,128)(2,1)S(1)} %add_convert_fusion), channel_id=1, source_target_pairs={{0,192},{16,208},{32,224},{48,240},{64,128},{80,144},{96,160},{112... | collective-permute-start | bytes 393224 | tf_op jit(solution)/shard_map/ppermute | solution.py:174
  46.1 7.4 %collective-permute-start.4 = (bf16[64,1024]{1,0:T(8,128)(2,1)S(1)}, bf16[64,1024]{1,0:T(8,128)(2,1)S(1)}, u32[]{:S(2)}, u32[]{:S(2)}) collective-permute-start(bf16[64,1024]{1,0:T(8,128)(2,1)S(1)} %add_convert_fusion.2), channel_id=1, source_target_pairs={{0,64},{16,80},{32,96},{48,112},{64,0},{80,16},{96,32},{112,48},{1... | collective-permute-start | bytes 393224 | tf_op jit(solution)/shard_map/ppermute | solution.py:174
  53.8 11.5 %collective-permute-start.17 = (bf16[64,1024]{1,0:T(8,128)(2,1)S(1)}, bf16[64,1024]{1,0:T(8,128)(2,1)S(1)}, u32[]{:S(2)}, u32[]{:S(2)}) collective-permute-start(bf16[64,1024]{1,0:T(8,128)(2,1)S(1)} %get-tuple-element.31.refs_0_), channel_id=1, source_target_pairs={{0,48},{16,0},{32,16},{48,32},{64,112},{80,64},{96,80},{112,96},{1... | collective-permute-start | bytes 393224 | tf_op jit(solution)/shard_map/ppermute | solution.py:184
  55.2 2.2 %copy-start.1 = (bf16[1,4,64,8192]{3,2,1,0:T(8,128)(2,1)S(1)}, bf16[1,4,64,8192]{3,2,1,0:T(8,128)(2,1)}, u32[]{:S(2)}) copy-start(bf16[1,4,64,8192]{3,2,1,0:T(8,128)(2,1)} %inner_ref.9) | copy-start | bytes 12582916
  57.4 10.8 %copy-start.2 = (bf16[1,4,64,8192]{3,2,1,0:T(8,128)(2,1)S(1)}, bf16[1,4,64,8192]{3,2,1,0:T(8,128)(2,1)}, u32[]{:S(2)}) copy-start(bf16[1,4,64,8192]{3,2,1,0:T(8,128)(2,1)} %inner_ref.9) | copy-start | bytes 12582916
  59.7 7.2 %collective-permute-start.16 = (bf16[64,1024]{1,0:T(8,128)(2,1)S(1)}, bf16[64,1024]{1,0:T(8,128)(2,1)S(1)}, u32[]{:S(2)}, u32[]{:S(2)}) collective-permute-start(bf16[64,1024]{1,0:T(8,128)(2,1)S(1)} %get-tuple-element.31.refs_0_), channel_id=1, source_target_pairs={{0,32},{16,48},{32,0},{48,16},{64,96},{80,112},{96,64},{112,80},{1... | collective-permute-start | bytes 393224 | tf_op jit(solution)/shard_map/ppermute | solution.py:184
  61.1 7.1 %collective-permute-start.15 = (bf16[64,1024]{1,0:T(8,128)(2,1)S(1)}, bf16[64,1024]{1,0:T(8,128)(2,1)S(1)}, u32[]{:S(2)}, u32[]{:S(2)}) collective-permute-start(bf16[64,1024]{1,0:T(8,128)(2,1)S(1)} %get-tuple-element.31.refs_0_), channel_id=1, source_target_pairs={{0,16},{16,32},{32,48},{48,0},{64,80},{80,96},{96,112},{112,64},{1... | collective-permute-start | bytes 393224 | tf_op jit(solution)/shard_map/ppermute | solution.py:184
  62.3 8.2 %collective-permute-start.9 = (bf16[64,1024]{1,0:T(8,128)(2,1)S(1)}, bf16[64,1024]{1,0:T(8,128)(2,1)S(1)}, u32[]{:S(2)}, u32[]{:S(2)}) collective-permute-start(bf16[64,1024]{1,0:T(8,128)(2,1)S(1)} %get-tuple-element.32.refs_0_), channel_id=1, source_target_pairs={{0,48},{16,0},{32,16},{48,32},{64,112},{80,64},{96,80},{112,96},{1... | collective-permute-start | bytes 393224 | tf_op jit(solution)/shard_map/ppermute | solution.py:184
  64.3 6.5 %collective-permute-start.8 = (bf16[64,1024]{1,0:T(8,128)(2,1)S(1)}, bf16[64,1024]{1,0:T(8,128)(2,1)S(1)}, u32[]{:S(2)}, u32[]{:S(2)}) collective-permute-start(bf16[64,1024]{1,0:T(8,128)(2,1)S(1)} %get-tuple-element.32.refs_0_), channel_id=1, source_target_pairs={{0,32},{16,48},{32,0},{48,16},{64,96},{80,112},{96,64},{112,80},{1... | collective-permute-start | bytes 393224 | tf_op jit(solution)/shard_map/ppermute | solution.py:184
  65.3 6.9 %collective-permute-start.7 = (bf16[64,1024]{1,0:T(8,128)(2,1)S(1)}, bf16[64,1024]{1,0:T(8,128)(2,1)S(1)}, u32[]{:S(2)}, u32[]{:S(2)}) collective-permute-start(bf16[64,1024]{1,0:T(8,128)(2,1)S(1)} %get-tuple-element.32.refs_0_), channel_id=1, source_target_pairs={{0,16},{16,32},{32,48},{48,0},{64,80},{80,96},{96,112},{112,64},{1... | collective-permute-start | bytes 393224 | tf_op jit(solution)/shard_map/ppermute | solution.py:184

commit v2 on v0

v2 whole, which is shorter than its diff:
```python
import functools

import jax
import jax.numpy as jnp
from jax import lax
from jax.experimental import pallas as pl
from jax.experimental.pallas import tpu as pltpu
from jax.sharding import PartitionSpec as P

momentum_coef = 0.9
outer_rate = 0.7
blend_keep = 0.5
grid_scale = 4.0
bit_levels = 4096.0

Y = 4
Z = 4
CHUNKS = 2
PER = Z // CHUNKS
PIECES = 2


def y_shift(k):
    return [(z * Y + y, z * Y + (y + k) % Y) for z in range(Z) for y in range(Y)]


def z_swap(s):
    return [(z * Y + y, (z ^ s) * Y + y) for z in range(Z) for y in range(Y)]


def pinned(x):
    return pltpu.with_memory_space_constraint(x, pltpu.HBM)


def round_kernel(chunk, share, ids, after_ref, inner_hbm, snap_hbm, bits_hbm, *refs):
    outs, snap_out, chosen = refs[:Y], refs[Y], refs[Y + 1]
    snaps, draws, sems = refs[Y + 2 :]
    rows = snaps.shape[0]
    wide = PER * Y * share
    strip = rows // PIECES
    cols = pl.ds(chunk * wide, wide)
    copies = []
    for p in range(PIECES):
        at = pl.ds(p * strip, strip)
        copies.append(
            [
                pltpu.make_async_copy(src, dst.at[at], sems.at[p, n])
                for n, (src, dst) in enumerate(
                    (
                        (bits_hbm.at[0, at, cols], draws),
                        (inner_hbm.at[0, ids[0], at, cols], chosen),
                        (snap_hbm.at[at, cols], snaps),
                    )
                )
            ]
        )
        for c in copies[-1]:
            c.start()
    for p in range(PIECES):
        for c in copies[p]:
            c.wait()
        for k in range(Y):
            owner = lax.rem(ids[1] + k, Y)
            for j in range(PER):
                for i in range(strip // 16):
                    at = pl.ds(p * strip + i * 16, 16)
                    block = pl.ds(pl.multiple_of((j * Y + owner) * share, share), share)
                    raw = snaps[at, block]
                    snap = grid_scale * raw.astype(jnp.float32)
                    kept = grid_scale * chosen[at, block].astype(jnp.float32)
                    level = draws[at, block].astype(jnp.float32) * (1.0 / bit_levels)
                    centred = jnp.ceil((snap - kept) - level) - jnp.floor(snap)
                    outs[k][at, j * share : (j + 1) * share] = centred.astype(jnp.bfloat16)
                    if k == 0:
                        snap_out[at, j * share : (j + 1) * share] = raw


def rounded_blocks(ids, after, inner, snapshot, bits, chunk, share):
    rows = snapshot.shape[0]
    wide = PER * Y * share
    return pl.pallas_call(
        functools.partial(round_kernel, chunk, share),
        out_shape=[pltpu.VMEM((rows, PER * share), jnp.bfloat16)] * (Y + 1)
        + [pltpu.VMEM((rows, wide), jnp.bfloat16)],
        in_specs=[pl.BlockSpec(memory_space=pltpu.SMEM)]
        + [pl.BlockSpec(memory_space=pl.ANY)]
        + [pl.BlockSpec(memory_space=pltpu.HBM)] * 3,
        out_specs=[pl.BlockSpec(memory_space=pltpu.VMEM)] * (Y + 2),
        scratch_shapes=[
            pltpu.VMEM((rows, wide), jnp.bfloat16),
            pltpu.VMEM((rows, wide), jnp.int32),
            pltpu.SemaphoreType.DMA((PIECES, 3)),
        ],
        compiler_params=pltpu.CompilerParams(vmem_limit_bytes=12 << 20),
        cost_estimate=pl.CostEstimate(
            flops=12 * rows * wide, bytes_accessed=10 * rows * wide, transcendentals=0
        ),
        name=f"round{chunk}",
    )(ids, after, pinned(inner), pinned(snapshot), pinned(bits))


def copy_kernel(ids, after_ref, inner_hbm, out_hbm, held, sems):
    frags = inner_hbm.shape[1]
    rows = inner_hbm.shape[2]
    strip = rows // PIECES
    steps = []
    for n in range(1, frags):
        f = lax.rem(ids[0] + n, frags)
        for p in range(PIECES):
            at = pl.ds(p * strip, strip)
            slot = held.at[n - 1, at]
            steps.append(
                (
                    pltpu.make_async_copy(inner_hbm.at[0, f, at], slot, sems.at[n - 1, p, 0]),
                    pltpu.make_async_copy(slot, out_hbm.at[0, f, at], sems.at[n - 1, p, 1]),
                )
            )
    for load, _ in steps:
        load.start()
    for load, store in steps:
        load.wait()
        store.start()
    for _, store in steps:
        store.wait()


def others_copied(ids, after, inner):
    frags = inner.shape[1]
    return pl.pallas_call(
        copy_kernel,
        out_shape=jax.ShapeDtypeStruct(inner.shape, inner.dtype),
        in_specs=[
            pl.BlockSpec(memory_space=pltpu.SMEM),
            pl.BlockSpec(memory_space=pl.ANY),
            pl.BlockSpec(memory_space=pltpu.HBM),
        ],
        out_specs=pl.BlockSpec(memory_space=pltpu.HBM),
        scratch_shapes=[
            pltpu.VMEM((frags - 1, *inner.shape[2:]), inner.dtype),
            pltpu.SemaphoreType.DMA((frags - 1, PIECES, 2)),
        ],
        compiler_params=pltpu.CompilerParams(vmem_limit_bytes=12 << 20),
        cost_estimate=pl.CostEstimate(flops=0, bytes_accessed=3 * inner.size, transcendentals=0),
        name="others",
    )(ids, after, pinned(inner))


def blend_kernel(chunk, share, ids, chosen, *refs):
    blocks = refs[:Y]
    snap_hbm, inner_out, snaps, mixed, sems = refs[-5:]
    rows = snaps.shape[0]
    wide = PER * Y * share
    strip = rows // PIECES
    cols = pl.ds(chunk * wide, wide)
    copies = []
    for p in range(PIECES):
        for k in range(Y):
            owner = lax.rem(ids[1] + Y - k, Y)
            for j in range(PER):
                for i in range(strip // 16):
                    at = pl.ds(p * strip + i * 16, 16)
                    block = pl.ds(pl.multiple_of((j * Y + owner) * share, share), share)
                    new = blocks[k][at, j * share : (j + 1) * share]
                    snaps[at, block] = new
                    mixed[at, block] = (
                        blend_keep * chosen[at, block].astype(jnp.float32)
                        + (1.0 - blend_keep) * new.astype(jnp.float32)
                    ).astype(jnp.bfloat16)
        at = pl.ds(p * strip, strip)
        copies += [
            pltpu.make_async_copy(snaps.at[at], snap_hbm.at[at, cols], sems.at[p, 0]),
            pltpu.make_async_copy(mixed.at[at], inner_out.at[0, ids[0], at, cols], sems.at[p, 1]),
        ]
        for c in copies[-2:]:
            c.start()
    for c in copies:
        c.wait()


def blended(ids, chosen, blocks, snap_out, inner_out, chunk, share):
    rows = blocks[0].shape[0]
    wide = PER * Y * share
    kept = [inner_out] if snap_out is None else [snap_out, inner_out]
    last = 1 + 1 + Y + len(kept) - 1
    aliases = {last: 1} if snap_out is None else {last - 1: 0, last: 1}
    hbm = pl.BlockSpec(memory_space=pltpu.HBM)
    return pl.pallas_call(
        functools.partial(blend_kernel, chunk, share),
        out_shape=[
            jax.ShapeDtypeStruct((rows, CHUNKS * wide), jnp.bfloat16),
            jax.ShapeDtypeStruct(inner_out.shape, inner_out.dtype),
        ],
        in_specs=[pl.BlockSpec(memory_space=pltpu.SMEM)]
        + [pl.BlockSpec(memory_space=pltpu.VMEM)] * (Y + 1)
        + [hbm] * len(kept),
        out_specs=[hbm, hbm],
        scratch_shapes=[pltpu.VMEM((rows, wide), jnp.bfloat16)] * 2
        + [pltpu.SemaphoreType.DMA((PIECES, 2))],
        input_output_aliases=aliases,
        compiler_params=pltpu.CompilerParams(vmem_limit_bytes=12 << 20),
        cost_estimate=pl.CostEstimate(
            flops=4 * rows * wide, bytes_accessed=8 * rows * wide, transcendentals=0
        ),
        name=f"blend{chunk}",
    )(ids, chosen, *blocks, *kept)


def body(inner, snapshot, momentum, bits, fragment):
    f32, bf16 = jnp.float32, jnp.bfloat16
    share = momentum.shape[1]
    me = lax.axis_index("replica")
    y, z = lax.rem(me, Y), lax.div(me, Y)
    ids = jnp.stack([fragment[0], y.astype(jnp.int32)])

    def send(x, perm):
        return lax.ppermute(x, "replica", perm)

    near = send(momentum, z_swap(1))
    odd = lax.rem(z, 2) == 1
    mine = [jnp.where(odd, near, momentum), jnp.where(odd, momentum, near)]
    both = jnp.concatenate(mine, axis=1)
    far = send(both, z_swap(3))
    far = [far[:, :share], far[:, share:]]
    high = lax.div(z, 2) == 1
    moments = [jnp.where(high, b, a) for a, b in zip(mine, far)]
    moments += [jnp.where(high, a, b) for a, b in zip(mine, far)]

    sent, parts, snaps, kept = [], [], [], []
    for c in range(CHUNKS):
        *blocks, snap, chosen = rounded_blocks(
            ids, ids if c == 0 else both, inner, snapshot, bits, c, share
        )
        sent.append(blocks)
        snaps.append(snap)
        kept.append(chosen)
    for c in range(CHUNKS):
        got = [sent[c][0]] + [send(sent[c][k], y_shift(k)) for k in range(1, Y)]
        parts.append(sum(g.astype(f32) for g in got).astype(bf16))
    others = others_copied(ids, moments[0], inner)
    grads, news = [], []
    for c in range(CHUNKS):
        order = (1, 3) if c % 2 == 0 else (3, 1)
        part = parts[c]
        part = (part.astype(f32) + send(part, z_swap(order[0])).astype(f32)).astype(bf16)
        if c == CHUNKS - 1:
            part, others = lax.optimization_barrier((part, others))
        total = part.astype(f32) + send(part, z_swap(order[1])).astype(f32)
        snap = snaps[c].astype(f32)
        grad = (total + (Y * Z) * jnp.floor(grid_scale * snap)) / (grid_scale * Y * Z)
        gathered = jnp.concatenate([moments[c * PER + j] for j in range(PER)], axis=1)
        moment = momentum_coef * gathered + grad
        grads.append(grad)
        news.append((snap - outer_rate * (grad + momentum_coef * moment)).astype(bf16))

    snap_out, inner_out = None, others
    for c in range(CHUNKS):
        blocks = [news[c]] + [send(news[c], y_shift(k)) for k in range(1, Y)]
        snap_out, inner_out = blended(ids, kept[c], blocks, snap_out, inner_out, c, share)

    own = grads[0][:, :share]
    for b in range(1, Z):
        at = (b % PER) * share
        own = jnp.where(z == b, grads[b // PER][:, at : at + share], own)
    return snap_out, momentum_coef * momentum + own, inner_out


def solution(mesh):
    placed = (
        P("replica", None, "fsdp", None),
        P("fsdp", None),
        P("fsdp", "replica"),
        P("replica", "fsdp", None),
        P(),
    )
    return jax.shard_map(
        body,
        mesh=mesh,
        in_specs=placed,
        out_specs=(P("fsdp", None), P("fsdp", "replica"), P("replica", None, "fsdp", None)),
        check_vma=False,
    )
```

time: 94 us -> 60 us (0.64)
  waiting for transfers between devices: 57 us -> 7.56 us
  starting transfers between devices: 17.1 us -> 38.4 us
  Pallas kernels: 0 us -> 11.1 us
  local copies, waits for them, and re-layouts: 9.19 us -> 0.01 us
  other arithmetic: 9.13 us -> 1.38 us
    all_to_all x2 -> x0, waiting for transfers between devices: 57 us -> none  [the longest x1 28.9 us: sent_to_all(): lax.all_to_all(jnp.broadcast_to(shard[None], (size, *shard.shape)), axis,...]
    ppermute x0 -> x18, starting transfers between devices: none -> 38.4 us  [send(): return lax.ppermute(x, 'replica', perm)]
    all_to_all x2 -> x0, starting transfers between devices: 17.1 us -> none  [the longest x1 11.3 us: sent_and_summed(): lax.all_to_all(blocks, axis, split_axis=0, concat_axis=0, tiled=True)]
    pallas_call x0 -> x5, Pallas kernels: none -> 11.1 us  [the longest x2 4.59 us: rounded_blocks(): pl.pallas_call(functools.partial(round_kernel, chunk, share), out_shape=[...]
    ppermute x0 -> x18, waiting for transfers between devices: none -> 7.56 us  [send(): return lax.ppermute(x, 'replica', perm)]
    convert_element_type x3 -> x4, other arithmetic: 4.84 us -> 0.22 us  [the longest x2 0.14 us: body(): parts.append(sum((g.astype(f32) for g in got)).astype(bf16))]
    convert_element_type x2 -> x0, local copies, waits for them, and re-layouts: 4.29 us -> none  [body(): new_snapshot.astype(jnp.float32)]
    select_n x1 -> x2, other arithmetic: 2.51 us -> 0.06 us  [the longest x1 0.04 us: body(): moments = [jnp.where(high, b, a) for a, b in zip(mine, far)]]
  transfers between devices with their start and end apart: 2 -> 18, of which waited for: 2 -> 7; matrix products, arithmetic and copies ran while one was open for 0% -> 2% of each run, Pallas kernels for 0% -> 16%
where the time goes in v2:
time: 60 us; the launch traced here: 59.8 us
  starting transfers between devices  38.4 us (64%)
  Pallas kernels  11.1 us (18%)
  waiting for transfers between devices  7.56 us (13%)
  between operations  1.39 us (2%)
  other arithmetic  1.38 us (2%)
    ppermute x18, starting transfers between devices, send(): return lax.ppermute(x, 'replica', perm)  38.4 us
    ppermute x18, waiting for transfers between devices, send(): return lax.ppermute(x, 'replica', perm)  7.56 us
    pallas_call x2, Pallas kernels, rounded_blocks(): pl.pallas_call(functools.partial(round_kernel, chunk, share), out_shape=[...  4.59 us
    pallas_call x1, Pallas kernels, others_copied(): pl.pallas_call(copy_kernel, out_shape=jax.ShapeDtypeStruct(inner.shape, i...  3.35 us
    pallas_call x2, Pallas kernels, blended(): pl.pallas_call(functools.partial(blend_kernel, chunk, share), out_shape=[...  3.14 us
  transfers between devices with their start and end apart: 18, of which 7 were waited for; matrix products, arithmetic and copies ran while one was open for 2% of the time, Pallas kernels for 16%

profile of v2, /device:TPU:2, one launch (start us, length us, event | category | flops | bytes accessed | tf_op | source)
XLA Modules:
  0.0 59.8 jit_solution(15109404586316481951)
XLA Ops:
  0.6 3.4 %collective-permute-start = (f32[64,512]{1,0:T(8,128)}, f32[64,512]{1,0:T(8,128)S(1)}, u32[]{:S(2)}, u32[]{:S(2)}) collective-permute-start(f32[64,512]{1,0:T(8,128)} %param.7), channel_id=1, source_target_pairs={{0,64},{16,80},{32,96},{48,112},{64,0},{80,16},{96,32},{112,48},{1... | collective-permute-start | bytes 393224 | tf_op jit(solution)/shard_map/ppermute | solution.py:216
  4.7 2.3 %round0.1 = (bf16[64,1024]{1,0:T(8,128)(2,1)S(1)}, bf16[64,1024]{1,0:T(8,128)(2,1)S(1)}, bf16[64,1024]{1,0:T(8,128)(2,1)S(1)}, bf16[64,1024]{1,0:T(8,128)(2,1)S(...) custom-call(s32[2]{0:T(128)S(1)} %pad_add_fusion.ids.after_ref, s32[2]{0:T(128)S(1)} %pad_add_fusion.ids.after_ref, ...), custom_call_target="tpu_custom_call" | custom-call | flops 3145728 | bytes 2621440 | tf_op jit(solution)/shard_map/round0/pallas_call | solution.py:81
  7.0 1.7 %collective-permute-start.10 = (bf16[64,1024]{1,0:T(8,128)(2,1)S(1)}, bf16[64,1024]{1,0:T(8,128)(2,1)S(1)}, u32[]{:S(2)}, u32[]{:S(2)}) collective-permute-start(bf16[64,1024]{1,0:T(8,128)(2,1)S(1)} %get-tuple-element.31), channel_id=1, source_target_pairs={{0,16},{16,32},{32,48},{48,0},{64,80},{80,96},{96,112},{112,64},{1... | collective-permute-start | bytes 393224 | tf_op jit(solution)/shard_map/ppermute | solution.py:216
  8.7 2.9 %collective-permute-start.11 = (bf16[64,1024]{1,0:T(8,128)(2,1)S(1)}, bf16[64,1024]{1,0:T(8,128)(2,1)S(1)}, u32[]{:S(2)}, u32[]{:S(2)}) collective-permute-start(bf16[64,1024]{1,0:T(8,128)(2,1)S(1)} %get-tuple-element.32), channel_id=1, source_target_pairs={{0,32},{16,48},{32,0},{48,16},{64,96},{80,112},{96,64},{112,80},{1... | collective-permute-start | bytes 393224 | tf_op jit(solution)/shard_map/ppermute | solution.py:216
  11.6 1.3 %collective-permute-start.12 = (bf16[64,1024]{1,0:T(8,128)(2,1)S(1)}, bf16[64,1024]{1,0:T(8,128)(2,1)S(1)}, u32[]{:S(2)}, u32[]{:S(2)}) collective-permute-start(bf16[64,1024]{1,0:T(8,128)(2,1)S(1)} %get-tuple-element.33), channel_id=1, source_target_pairs={{0,48},{16,0},{32,16},{48,32},{64,112},{80,64},{96,80},{112,96},{1... | collective-permute-start | bytes 393224 | tf_op jit(solution)/shard_map/ppermute | solution.py:216
  13.0 4.6 %collective-permute-start.5 = (f32[64,1024]{1,0:T(8,128)S(1)}, f32[64,1024]{1,0:T(8,128)S(1)}, u32[]{:S(2)}, u32[]{:S(2)}) collective-permute-start(f32[64,1024]{1,0:T(8,128)S(1)} %pad_maximum_fusion.after_ref), channel_id=1, source_target_pairs={{0,192},{16,208},{32,224},{48,240},{64,128},{80,144},{96,160},{112... | collective-permute-start | bytes 786440 | tf_op jit(solution)/shard_map/ppermute | solution.py:216
  17.6 2.3 %round1.1 = (bf16[64,1024]{1,0:T(8,128)(2,1)S(1)}, bf16[64,1024]{1,0:T(8,128)(2,1)S(1)}, bf16[64,1024]{1,0:T(8,128)(2,1)S(1)}, bf16[64,1024]{1,0:T(8,128)(2,1)S(...) custom-call(s32[2]{0:T(128)S(1)} %pad_add_fusion.ids.after_ref, ...), custom_call_target="tpu_custom_call" | custom-call | flops 3145728 | bytes 2621440 | tf_op jit(solution)/shard_map/round1/pallas_call | solution.py:81
  21.4 2.0 %collective-permute-start.3 = (bf16[64,1024]{1,0:T(8,128)(2,1)S(1)}, bf16[64,1024]{1,0:T(8,128)(2,1)S(1)}, u32[]{:S(2)}, u32[]{:S(2)}) collective-permute-start(bf16[64,1024]{1,0:T(8,128)(2,1)S(1)} %get-tuple-element.26), channel_id=1, source_target_pairs={{0,48},{16,0},{32,16},{48,32},{64,112},{80,64},{96,80},{112,96},{1... | collective-permute-start | bytes 393224 | tf_op jit(solution)/shard_map/ppermute | solution.py:216
  23.5 2.7 %collective-permute-start.13 = (bf16[64,1024]{1,0:T(8,128)(2,1)S(1)}, bf16[64,1024]{1,0:T(8,128)(2,1)S(1)}, u32[]{:S(2)}, u32[]{:S(2)}) collective-permute-start(bf16[64,1024]{1,0:T(8,128)(2,1)S(1)} %add_convert_fusion.1), channel_id=1, source_target_pairs={{0,64},{16,80},{32,96},{48,112},{64,0},{80,16},{96,32},{112,48},{1... | collective-permute-start | bytes 393224 | tf_op jit(solution)/shard_map/ppermute | solution.py:216
  26.2 1.8 %collective-permute-done.1 = bf16[64,1024]{1,0:T(8,128)(2,1)S(1)} collective-permute-done((bf16[64,1024]{1,0:T(8,128)(2,1)S(1)}, bf16[64,1024]{1,0:T(8,128)(2,1)S(1)}, u32[]{:S(2)}, u32[]{:S(2)}) %collective-permute-start.1) | collective-permute-done | bytes 131104 | tf_op jit(solution)/shard_map/ppermute | solution.py:216
  28.9 1.1 %collective-permute-done.13 = bf16[64,1024]{1,0:T(8,128)(2,1)S(1)} collective-permute-done((bf16[64,1024]{1,0:T(8,128)(2,1)S(1)}, bf16[64,1024]{1,0:T(8,128)(2,1)S(1)}, u32[]{:S(2)}, u32[]{:S(2)}) %collective-permute-start.13) | collective-permute-done | bytes 131104 | tf_op jit(solution)/shard_map/ppermute | solution.py:216
  30.0 4.4 %collective-permute-start.14 = (bf16[64,1024]{1,0:T(8,128)(2,1)S(1)}, bf16[64,1024]{1,0:T(8,128)(2,1)S(1)}, u32[]{:S(2)}, u32[]{:S(2)}) collective-permute-start(bf16[64,1024]{1,0:T(8,128)(2,1)S(1)} %add_convert_fusion), channel_id=1, source_target_pairs={{0,192},{16,208},{32,224},{48,240},{64,128},{80,144},{96,160},{112... | collective-permute-start | bytes 393224 | tf_op jit(solution)/shard_map/ppermute | solution.py:216
  34.5 3.3 %others.1.refs_4_ = bf16[1,4,64,8192]{3,2,1,0:T(8,128)(2,1)} custom-call(s32[2]{0:T(128)S(1)} %pad_add_fusion.ids.after_ref, f32[64,512]{1,0:T(8,128)S(1)} %get-tuple-element.48.after_ref, bf16[1,4,64,8192]{3,2,1,0:T(8,128)(2,1)} %inner_hbm.5), custom_call_target="tpu_custom_call" | custom-call | bytes 6291456 | tf_op jit(solution)/shard_map/others/pallas_call | solution.py:129
  37.9 1.6 %collective-permute-start.6 = (bf16[64,1024]{1,0:T(8,128)(2,1)S(1)}, bf16[64,1024]{1,0:T(8,128)(2,1)S(1)}, u32[]{:S(2)}, u32[]{:S(2)}) collective-permute-start(bf16[64,1024]{1,0:T(8,128)(2,1)S(1)} %add_convert_fusion.2), channel_id=1, source_target_pairs={{0,64},{16,80},{32,96},{48,112},{64,0},{80,16},{96,32},{112,48},{1... | collective-permute-start | bytes 393224 | tf_op jit(solution)/shard_map/ppermute | solution.py:216
  39.6 6.3 %collective-permute-start.17 = (bf16[64,1024]{1,0:T(8,128)(2,1)S(1)}, bf16[64,1024]{1,0:T(8,128)(2,1)S(1)}, u32[]{:S(2)}, u32[]{:S(2)}) collective-permute-start(bf16[64,1024]{1,0:T(8,128)(2,1)S(1)} %get-tuple-element.42.refs_0_), channel_id=1, source_target_pairs={{0,48},{16,0},{32,16},{48,32},{64,112},{80,64},{96,80},{112,96},{1... | collective-permute-start | bytes 393224 | tf_op jit(solution)/shard_map/ppermute | solution.py:216
  46.0 1.0 %collective-permute-start.15 = (bf16[64,1024]{1,0:T(8,128)(2,1)S(1)}, bf16[64,1024]{1,0:T(8,128)(2,1)S(1)}, u32[]{:S(2)}, u32[]{:S(2)}) collective-permute-start(bf16[64,1024]{1,0:T(8,128)(2,1)S(1)} %get-tuple-element.42.refs_0_), channel_id=1, source_target_pairs={{0,16},{16,32},{32,48},{48,0},{64,80},{80,96},{96,112},{112,64},{1... | collective-permute-start | bytes 393224 | tf_op jit(solution)/shard_map/ppermute | solution.py:216
  47.1 3.3 %collective-permute-start.9 = (bf16[64,1024]{1,0:T(8,128)(2,1)S(1)}, bf16[64,1024]{1,0:T(8,128)(2,1)S(1)}, u32[]{:S(2)}, u32[]{:S(2)}) collective-permute-start(bf16[64,1024]{1,0:T(8,128)(2,1)S(1)} %get-tuple-element.40.refs_0_), channel_id=1, source_target_pairs={{0,48},{16,0},{32,16},{48,32},{64,112},{80,64},{96,80},{112,96},{1... | collective-permute-start | bytes 393224 | tf_op jit(solution)/shard_map/ppermute | solution.py:216
  50.3 1.4 %collective-permute-start.8 = (bf16[64,1024]{1,0:T(8,128)(2,1)S(1)}, bf16[64,1024]{1,0:T(8,128)(2,1)S(1)}, u32[]{:S(2)}, u32[]{:S(2)}) collective-permute-start(bf16[64,1024]{1,0:T(8,128)(2,1)S(1)} %get-tuple-element.40.refs_0_), channel_id=1, source_target_pairs={{0,32},{16,48},{32,0},{48,16},{64,96},{80,112},{96,64},{112,80},{1... | collective-permute-start | bytes 393224 | tf_op jit(solution)/shard_map/ppermute | solution.py:216
  51.7 1.0 %collective-permute-done.16.refs_2_ = bf16[64,1024]{1,0:T(8,128)(2,1)S(1)} collective-permute-done((bf16[64,1024]{1,0:T(8,128)(2,1)S(1)}, bf16[64,1024]{1,0:T(8,128)(2,1)S(1)}, u32[]{:S(2)}, u32[]{:S(2)}) %collective-permute-start.16) | collective-permute-done | bytes 131104 | tf_op jit(solution)/shard_map/ppermute | solution.py:216
  52.8 0.9 %collective-permute-done.15.refs_1_ = bf16[64,1024]{1,0:T(8,128)(2,1)S(1)} collective-permute-done((bf16[64,1024]{1,0:T(8,128)(2,1)S(1)}, bf16[64,1024]{1,0:T(8,128)(2,1)S(1)}, u32[]{:S(2)}, u32[]{:S(2)}) %collective-permute-start.15) | collective-permute-done | bytes 131104 | tf_op jit(solution)/shard_map/ppermute | solution.py:216
  53.7 1.6 %blend0.1 = (bf16[64,8192]{1,0:T(8,128)(2,1)}, bf16[1,4,64,8192]{3,2,1,0:T(8,128)(2,1)}) custom-call(s32[2]{0:T(128)S(1)} %pad_add_fusion.ids.after_ref, bf16[64,4096]{1,0:T(8,128)(2,1)S(1)} %get-tuple-element.28.chosen, bf16[64,1024]{1,0:T(8,128)(2,1)S(1)} %get-tuple-element.42.refs_0_, ...), custom_call_target="tpu_custom_call", output_to_operand_aliasing={{1}: (6, {})} | custom-call | flops 1048576 | bytes 2097152 | tf_op jit(solution)/shard_map/blend0/pallas_call | solution.py:187
  56.0 0.8 %collective-permute-done.8.refs_2_ = bf16[64,1024]{1,0:T(8,128)(2,1)S(1)} collective-permute-done((bf16[64,1024]{1,0:T(8,128)(2,1)S(1)}, bf16[64,1024]{1,0:T(8,128)(2,1)S(1)}, u32[]{:S(2)}, u32[]{:S(2)}) %collective-permute-start.8) | collective-permute-done | bytes 131104 | tf_op jit(solution)/shard_map/ppermute | solution.py:216
  56.8 1.4 %collective-permute-done.7.refs_1_ = bf16[64,1024]{1,0:T(8,128)(2,1)S(1)} collective-permute-done((bf16[64,1024]{1,0:T(8,128)(2,1)S(1)}, bf16[64,1024]{1,0:T(8,128)(2,1)S(1)}, u32[]{:S(2)}, u32[]{:S(2)}) %collective-permute-start.7) | collective-permute-done | bytes 131104 | tf_op jit(solution)/shard_map/ppermute | solution.py:216
  58.2 1.6 %blend1.1 = (bf16[64,8192]{1,0:T(8,128)(2,1)}, bf16[1,4,64,8192]{3,2,1,0:T(8,128)(2,1)}) custom-call(s32[2]{0:T(128)S(1)} %pad_add_fusion.ids.after_ref, bf16[64,4096]{1,0:T(8,128)(2,1)S(1)} %get-tuple-element.21.chosen, bf16[64,1024]{1,0:T(8,128)(2,1)S(1)} %get-tuple-element.40.refs_0_, ...), custom_call_target="tpu_custom_call", output_to_operand_aliasing={{0}: (6, {}), {1}: (7, {})} | custom-call | flops 1048576 | bytes 2097152 | tf_op jit(solution)/shard_map/blend1/pallas_call | solution.py:187
  (30 shorter events, 3.8 us)
Async XLA Ops:
  0.6 12.3 %copy-start = (f32[64,512]{1,0:T(8,128)S(1)}, f32[64,512]{1,0:T(8,128)}, u32[]{:S(2)}) copy-start(f32[64,512]{1,0:T(8,128)} %param.7) | copy-start | bytes 393220
  0.6 12.3 %collective-permute-start = (f32[64,512]{1,0:T(8,128)}, f32[64,512]{1,0:T(8,128)S(1)}, u32[]{:S(2)}, u32[]{:S(2)}) collective-permute-start(f32[64,512]{1,0:T(8,128)} %param.7), channel_id=1, source_target_pairs={{0,64},{16,80},{32,96},{48,112},{64,0},{80,16},{96,32},{112,48},{1... | collective-permute-start | bytes 393224 | tf_op jit(solution)/shard_map/ppermute | solution.py:216
  7.0 13.6 %collective-permute-start.10 = (bf16[64,1024]{1,0:T(8,128)(2,1)S(1)}, bf16[64,1024]{1,0:T(8,128)(2,1)S(1)}, u32[]{:S(2)}, u32[]{:S(2)}) collective-permute-start(bf16[64,1024]{1,0:T(8,128)(2,1)S(1)} %get-tuple-element.31), channel_id=1, source_target_pairs={{0,16},{16,32},{32,48},{48,0},{64,80},{80,96},{96,112},{112,64},{1... | collective-permute-start | bytes 393224 | tf_op jit(solution)/shard_map/ppermute | solution.py:216
  8.7 12.7 %collective-permute-start.11 = (bf16[64,1024]{1,0:T(8,128)(2,1)S(1)}, bf16[64,1024]{1,0:T(8,128)(2,1)S(1)}, u32[]{:S(2)}, u32[]{:S(2)}) collective-permute-start(bf16[64,1024]{1,0:T(8,128)(2,1)S(1)} %get-tuple-element.32), channel_id=1, source_target_pairs={{0,32},{16,48},{32,0},{48,16},{64,96},{80,112},{96,64},{112,80},{1... | collective-permute-start | bytes 393224 | tf_op jit(solution)/shard_map/ppermute | solution.py:216
  11.6 11.8 %collective-permute-start.12 = (bf16[64,1024]{1,0:T(8,128)(2,1)S(1)}, bf16[64,1024]{1,0:T(8,128)(2,1)S(1)}, u32[]{:S(2)}, u32[]{:S(2)}) collective-permute-start(bf16[64,1024]{1,0:T(8,128)(2,1)S(1)} %get-tuple-element.33), channel_id=1, source_target_pairs={{0,48},{16,0},{32,16},{48,32},{64,112},{80,64},{96,80},{112,96},{1... | collective-permute-start | bytes 393224 | tf_op jit(solution)/shard_map/ppermute | solution.py:216
  13.0 21.5 %collective-permute-start.5 = (f32[64,1024]{1,0:T(8,128)S(1)}, f32[64,1024]{1,0:T(8,128)S(1)}, u32[]{:S(2)}, u32[]{:S(2)}) collective-permute-start(f32[64,1024]{1,0:T(8,128)S(1)} %pad_maximum_fusion.after_ref), channel_id=1, source_target_pairs={{0,192},{16,208},{32,224},{48,240},{64,128},{80,144},{96,160},{112... | collective-permute-start | bytes 786440 | tf_op jit(solution)/shard_map/ppermute | solution.py:216
  19.9 8.1 %collective-permute-start.1 = (bf16[64,1024]{1,0:T(8,128)(2,1)S(1)}, bf16[64,1024]{1,0:T(8,128)(2,1)S(1)}, u32[]{:S(2)}, u32[]{:S(2)}) collective-permute-start(bf16[64,1024]{1,0:T(8,128)(2,1)S(1)} %get-tuple-element.24), channel_id=1, source_target_pairs={{0,16},{16,32},{32,48},{48,0},{64,80},{80,96},{96,112},{112,64},{1... | collective-permute-start | bytes 393224 | tf_op jit(solution)/shard_map/ppermute | solution.py:216
  20.6 7.4 %collective-permute-start.2 = (bf16[64,1024]{1,0:T(8,128)(2,1)S(1)}, bf16[64,1024]{1,0:T(8,128)(2,1)S(1)}, u32[]{:S(2)}, u32[]{:S(2)}) collective-permute-start(bf16[64,1024]{1,0:T(8,128)(2,1)S(1)} %get-tuple-element.25), channel_id=1, source_target_pairs={{0,32},{16,48},{32,0},{48,16},{64,96},{80,112},{96,64},{112,80},{1... | collective-permute-start | bytes 393224 | tf_op jit(solution)/shard_map/ppermute | solution.py:216
  21.4 7.0 %collective-permute-start.3 = (bf16[64,1024]{1,0:T(8,128)(2,1)S(1)}, bf16[64,1024]{1,0:T(8,128)(2,1)S(1)}, u32[]{:S(2)}, u32[]{:S(2)}) collective-permute-start(bf16[64,1024]{1,0:T(8,128)(2,1)S(1)} %get-tuple-element.26), channel_id=1, source_target_pairs={{0,48},{16,0},{32,16},{48,32},{64,112},{80,64},{96,80},{112,96},{1... | collective-permute-start | bytes 393224 | tf_op jit(solution)/shard_map/ppermute | solution.py:216
  23.5 6.5 %collective-permute-start.13 = (bf16[64,1024]{1,0:T(8,128)(2,1)S(1)}, bf16[64,1024]{1,0:T(8,128)(2,1)S(1)}, u32[]{:S(2)}, u32[]{:S(2)}) collective-permute-start(bf16[64,1024]{1,0:T(8,128)(2,1)S(1)} %add_convert_fusion.1), channel_id=1, source_target_pairs={{0,64},{16,80},{32,96},{48,112},{64,0},{80,16},{96,32},{112,48},{1... | collective-permute-start | bytes 393224 | tf_op jit(solution)/shard_map/ppermute | solution.py:216
  28.5 9.3 %collective-permute-start.4 = (bf16[64,1024]{1,0:T(8,128)(2,1)S(1)}, bf16[64,1024]{1,0:T(8,128)(2,1)S(1)}, u32[]{:S(2)}, u32[]{:S(2)}) collective-permute-start(bf16[64,1024]{1,0:T(8,128)(2,1)S(1)} %add_convert_fusion.3), channel_id=1, source_target_pairs={{0,192},{16,208},{32,224},{48,240},{64,128},{80,144},{96,160},{112... | collective-permute-start | bytes 393224 | tf_op jit(solution)/shard_map/ppermute | solution.py:216
  30.0 9.5 %collective-permute-start.14 = (bf16[64,1024]{1,0:T(8,128)(2,1)S(1)}, bf16[64,1024]{1,0:T(8,128)(2,1)S(1)}, u32[]{:S(2)}, u32[]{:S(2)}) collective-permute-start(bf16[64,1024]{1,0:T(8,128)(2,1)S(1)} %add_convert_fusion), channel_id=1, source_target_pairs={{0,192},{16,208},{32,224},{48,240},{64,128},{80,144},{96,160},{112... | collective-permute-start | bytes 393224 | tf_op jit(solution)/shard_map/ppermute | solution.py:216
  37.9 9.0 %collective-permute-start.6 = (bf16[64,1024]{1,0:T(8,128)(2,1)S(1)}, bf16[64,1024]{1,0:T(8,128)(2,1)S(1)}, u32[]{:S(2)}, u32[]{:S(2)}) collective-permute-start(bf16[64,1024]{1,0:T(8,128)(2,1)S(1)} %add_convert_fusion.2), channel_id=1, source_target_pairs={{0,64},{16,80},{32,96},{48,112},{64,0},{80,16},{96,32},{112,48},{1... | collective-permute-start | bytes 393224 | tf_op jit(solution)/shard_map/ppermute | solution.py:216
  39.6 12.1 %collective-permute-start.17 = (bf16[64,1024]{1,0:T(8,128)(2,1)S(1)}, bf16[64,1024]{1,0:T(8,128)(2,1)S(1)}, u32[]{:S(2)}, u32[]{:S(2)}) collective-permute-start(bf16[64,1024]{1,0:T(8,128)(2,1)S(1)} %get-tuple-element.42.refs_0_), channel_id=1, source_target_pairs={{0,48},{16,0},{32,16},{48,32},{64,112},{80,64},{96,80},{112,96},{1... | collective-permute-start | bytes 393224 | tf_op jit(solution)/shard_map/ppermute | solution.py:216
  46.0 6.8 %collective-permute-start.16 = (bf16[64,1024]{1,0:T(8,128)(2,1)S(1)}, bf16[64,1024]{1,0:T(8,128)(2,1)S(1)}, u32[]{:S(2)}, u32[]{:S(2)}) collective-permute-start(bf16[64,1024]{1,0:T(8,128)(2,1)S(1)} %get-tuple-element.42.refs_0_), channel_id=1, source_target_pairs={{0,32},{16,48},{32,0},{48,16},{64,96},{80,112},{96,64},{112,80},{1... | collective-permute-start | bytes 393224 | tf_op jit(solution)/shard_map/ppermute | solution.py:216
  46.0 7.8 %collective-permute-start.15 = (bf16[64,1024]{1,0:T(8,128)(2,1)S(1)}, bf16[64,1024]{1,0:T(8,128)(2,1)S(1)}, u32[]{:S(2)}, u32[]{:S(2)}) collective-permute-start(bf16[64,1024]{1,0:T(8,128)(2,1)S(1)} %get-tuple-element.42.refs_0_), channel_id=1, source_target_pairs={{0,16},{16,32},{32,48},{48,0},{64,80},{80,96},{96,112},{112,64},{1... | collective-permute-start | bytes 393224 | tf_op jit(solution)/shard_map/ppermute | solution.py:216
  47.1 8.9 %collective-permute-start.9 = (bf16[64,1024]{1,0:T(8,128)(2,1)S(1)}, bf16[64,1024]{1,0:T(8,128)(2,1)S(1)}, u32[]{:S(2)}, u32[]{:S(2)}) collective-permute-start(bf16[64,1024]{1,0:T(8,128)(2,1)S(1)} %get-tuple-element.40.refs_0_), channel_id=1, source_target_pairs={{0,48},{16,0},{32,16},{48,32},{64,112},{80,64},{96,80},{112,96},{1... | collective-permute-start | bytes 393224 | tf_op jit(solution)/shard_map/ppermute | solution.py:216
  50.3 6.5 %collective-permute-start.8 = (bf16[64,1024]{1,0:T(8,128)(2,1)S(1)}, bf16[64,1024]{1,0:T(8,128)(2,1)S(1)}, u32[]{:S(2)}, u32[]{:S(2)}) collective-permute-start(bf16[64,1024]{1,0:T(8,128)(2,1)S(1)} %get-tuple-element.40.refs_0_), channel_id=1, source_target_pairs={{0,32},{16,48},{32,0},{48,16},{64,96},{80,112},{96,64},{112,80},{1... | collective-permute-start | bytes 393224 | tf_op jit(solution)/shard_map/ppermute | solution.py:216
  51.7 6.5 %collective-permute-start.7 = (bf16[64,1024]{1,0:T(8,128)(2,1)S(1)}, bf16[64,1024]{1,0:T(8,128)(2,1)S(1)}, u32[]{:S(2)}, u32[]{:S(2)}) collective-permute-start(bf16[64,1024]{1,0:T(8,128)(2,1)S(1)} %get-tuple-element.40.refs_0_), channel_id=1, source_target_pairs={{0,16},{16,32},{32,48},{48,0},{64,80},{80,96},{96,112},{112,64},{1... | collective-permute-start | bytes 393224 | tf_op jit(solution)/shard_map/ppermute | solution.py:216

commit v3 on v2

--- a/solution.py
+++ b/solution.py
@@ -18,6 +18,7 @@
 CHUNKS = 2
 PER = Z // CHUNKS
 PIECES = 2
+ORDER = (0, 3, 1, 2)
 
 
 def y_shift(k):
@@ -26,6 +27,10 @@
 
 def z_swap(s):
     return [(z * Y + y, (z ^ s) * Y + y) for z in range(Z) for y in range(Y)]
+
+
+def here():
+    return lax.rem(lax.axis_index("replica"), Y)
 
 
 def pinned(x):
@@ -60,7 +65,7 @@
         for c in copies[p]:
             c.wait()
         for k in range(Y):
-            owner = lax.rem(ids[1] + k, Y)
+            owner = lax.rem(here() + k, Y)
             for j in range(PER):
                 for i in range(strip // 16):
                     at = pl.ds(p * strip + i * 16, 16)
@@ -154,13 +159,13 @@
     cols = pl.ds(chunk * wide, wide)
     copies = []
     for p in range(PIECES):
-        for k in range(Y):
-            owner = lax.rem(ids[1] + Y - k, Y)
+        for n, k in enumerate(ORDER):
+            owner = lax.rem(here() + Y - k, Y)
             for j in range(PER):
                 for i in range(strip // 16):
                     at = pl.ds(p * strip + i * 16, 16)
                     block = pl.ds(pl.multiple_of((j * Y + owner) * share, share), share)
-                    new = blocks[k][at, j * share : (j + 1) * share]
+                    new = blocks[n][at, j * share : (j + 1) * share]
                     snaps[at, block] = new
                     mixed[at, block] = (
                         blend_keep * chosen[at, block].astype(jnp.float32)
@@ -210,7 +215,7 @@
     share = momentum.shape[1]
     me = lax.axis_index("replica")
     y, z = lax.rem(me, Y), lax.div(me, Y)
-    ids = jnp.stack([fragment[0], y.astype(jnp.int32)])
+    ids = fragment
 
     def send(x, perm):
         return lax.ppermute(x, "replica", perm)
@@ -234,7 +239,7 @@
         snaps.append(snap)
         kept.append(chosen)
     for c in range(CHUNKS):
-        got = [sent[c][0]] + [send(sent[c][k], y_shift(k)) for k in range(1, Y)]
+        got = [sent[c][0]] + [send(sent[c][k], y_shift(k)) for k in (2, 1, 3)]
         parts.append(sum(g.astype(f32) for g in got).astype(bf16))
     others = others_copied(ids, moments[0], inner)
     grads, news = [], []
@@ -254,7 +259,7 @@
 
     snap_out, inner_out = None, others
     for c in range(CHUNKS):
-        blocks = [news[c]] + [send(news[c], y_shift(k)) for k in range(1, Y)]
+        blocks = [news[c]] + [send(news[c], y_shift(k)) for k in ORDER[1:]]
         snap_out, inner_out = blended(ids, kept[c], blocks, snap_out, inner_out, c, share)
 
     own = grads[0][:, :share]

time: 60 us -> 58.4 us (0.973); the launches traced: 59.8 us -> 57.4 us
  Pallas kernels: 11.1 us -> 8.4 us
  starting transfers between devices: 38.4 us -> 39.5 us
  waiting for transfers between devices: 7.56 us -> 6.84 us
    ppermute x18, starting transfers between devices: 38.4 us -> 39.5 us  [send(): return lax.ppermute(x, 'replica', perm)]
    pallas_call x2, Pallas kernels: 4.59 us -> 3.51 us  [rounded_blocks(): pl.pallas_call(functools.partial(round_kernel, chunk, share), out_shape=[...]
    pallas_call x2, Pallas kernels: 3.14 us -> 2.08 us  [blended(): pl.pallas_call(functools.partial(blend_kernel, chunk, share), out_shape=[...]
    ppermute x18, waiting for transfers between devices: 7.56 us -> 6.84 us  [send(): return lax.ppermute(x, 'replica', perm)]
  transfers between devices with their start and end apart: 18 -> 18, of which waited for: 7 -> 6; matrix products, arithmetic and copies ran while one was open for 2% -> 2% of each run, Pallas kernels for 16% -> 13%
where the time goes in v3:
time: 58.4 us; the launch traced here: 57.4 us
  starting transfers between devices  39.5 us (68%)
  Pallas kernels  8.4 us (14%)
  waiting for transfers between devices  6.84 us (12%)
  between operations  1.39 us (2%)
  other arithmetic  1.29 us (2%)
    ppermute x18, starting transfers between devices, send(): return lax.ppermute(x, 'replica', perm)  39.5 us
    ppermute x18, waiting for transfers between devices, send(): return lax.ppermute(x, 'replica', perm)  6.84 us
    pallas_call x2, Pallas kernels, rounded_blocks(): pl.pallas_call(functools.partial(round_kernel, chunk, share), out_shape=[...  3.51 us
    pallas_call x1, Pallas kernels, others_copied(): pl.pallas_call(copy_kernel, out_shape=jax.ShapeDtypeStruct(inner.shape, i...  2.81 us
    pallas_call x2, Pallas kernels, blended(): pl.pallas_call(functools.partial(blend_kernel, chunk, share), out_shape=[...  2.08 us
  transfers between devices with their start and end apart: 18, of which 6 were waited for; matrix products, arithmetic and copies ran while one was open for 2% of the time, Pallas kernels for 13%

profile of v3, /device:TPU:2, one launch (start us, length us, event | category | flops | bytes accessed | tf_op | source)
XLA Modules:
  0.0 57.4 jit_solution(6175962723928898012)
XLA Ops:
  0.6 3.4 %collective-permute-start = (f32[64,512]{1,0:T(8,128)}, f32[64,512]{1,0:T(8,128)S(1)}, u32[]{:S(2)}, u32[]{:S(2)}) collective-permute-start(f32[64,512]{1,0:T(8,128)} %param.7), channel_id=1, source_target_pairs={{0,64},{16,80},{32,96},{48,112},{64,0},{80,16},{96,32},{112,48},{1... | collective-permute-start | bytes 393224 | tf_op jit(solution)/shard_map/ppermute | solution.py:221
  4.6 1.8 %round0.1 = (bf16[64,1024]{1,0:T(8,128)(2,1)S(1)}, bf16[64,1024]{1,0:T(8,128)(2,1)S(1)}, bf16[64,1024]{1,0:T(8,128)(2,1)S(1)}, bf16[64,1024]{1,0:T(8,128)(2,1)S(...) custom-call(s32[1]{0:T(128)S(6)} %copy.14.ids.after_ref, s32[1]{0:T(128)S(6)} %copy.14.ids.after_ref, ...), custom_call_target="tpu_custom_call" | custom-call | flops 3145728 | bytes 2621440 | tf_op jit(solution)/shard_map/round0/pallas_call | solution.py:86
  6.4 3.3 %collective-permute-start.10 = (bf16[64,1024]{1,0:T(8,128)(2,1)S(1)}, bf16[64,1024]{1,0:T(8,128)(2,1)S(1)}, u32[]{:S(2)}, u32[]{:S(2)}) collective-permute-start(bf16[64,1024]{1,0:T(8,128)(2,1)S(1)} %get-tuple-element.31), channel_id=1, source_target_pairs={{0,32},{16,48},{32,0},{48,16},{64,96},{80,112},{96,64},{112,80},{1... | collective-permute-start | bytes 393224 | tf_op jit(solution)/shard_map/ppermute | solution.py:221
  10.4 2.6 %collective-permute-start.12 = (bf16[64,1024]{1,0:T(8,128)(2,1)S(1)}, bf16[64,1024]{1,0:T(8,128)(2,1)S(1)}, u32[]{:S(2)}, u32[]{:S(2)}) collective-permute-start(bf16[64,1024]{1,0:T(8,128)(2,1)S(1)} %get-tuple-element.33), channel_id=1, source_target_pairs={{0,48},{16,0},{32,16},{48,32},{64,112},{80,64},{96,80},{112,96},{1... | collective-permute-start | bytes 393224 | tf_op jit(solution)/shard_map/ppermute | solution.py:221
  13.0 4.6 %collective-permute-start.5 = (f32[64,1024]{1,0:T(8,128)S(1)}, f32[64,1024]{1,0:T(8,128)S(1)}, u32[]{:S(2)}, u32[]{:S(2)}) collective-permute-start(f32[64,1024]{1,0:T(8,128)S(1)} %pad_maximum_fusion.after_ref), channel_id=1, source_target_pairs={{0,192},{16,208},{32,224},{48,240},{64,128},{80,144},{96,160},{112... | collective-permute-start | bytes 786440 | tf_op jit(solution)/shard_map/ppermute | solution.py:221
  17.6 1.8 %round1.1 = (bf16[64,1024]{1,0:T(8,128)(2,1)S(1)}, bf16[64,1024]{1,0:T(8,128)(2,1)S(1)}, bf16[64,1024]{1,0:T(8,128)(2,1)S(1)}, bf16[64,1024]{1,0:T(8,128)(2,1)S(...) custom-call(s32[1]{0:T(128)S(6)} %copy.14.ids.after_ref, f32[64,1024]{1,0:T(8,128)S(1)} %pad_maximum_fusion.after_ref, ...), custom_call_target="tpu_custom_call" | custom-call | flops 3145728 | bytes 2621440 | tf_op jit(solution)/shard_map/round1/pallas_call | solution.py:86
  20.3 2.5 %collective-permute-start.3 = (bf16[64,1024]{1,0:T(8,128)(2,1)S(1)}, bf16[64,1024]{1,0:T(8,128)(2,1)S(1)}, u32[]{:S(2)}, u32[]{:S(2)}) collective-permute-start(bf16[64,1024]{1,0:T(8,128)(2,1)S(1)} %get-tuple-element.26), channel_id=1, source_target_pairs={{0,48},{16,0},{32,16},{48,32},{64,112},{80,64},{96,80},{112,96},{1... | collective-permute-start | bytes 393224 | tf_op jit(solution)/shard_map/ppermute | solution.py:221
  22.9 3.4 %collective-permute-start.13 = (bf16[64,1024]{1,0:T(8,128)(2,1)S(1)}, bf16[64,1024]{1,0:T(8,128)(2,1)S(1)}, u32[]{:S(2)}, u32[]{:S(2)}) collective-permute-start(bf16[64,1024]{1,0:T(8,128)(2,1)S(1)} %add_convert_fusion.1), channel_id=1, source_target_pairs={{0,64},{16,80},{32,96},{48,112},{64,0},{80,16},{96,32},{112,48},{1... | collective-permute-start | bytes 393224 | tf_op jit(solution)/shard_map/ppermute | solution.py:221
  26.3 1.3 %collective-permute-done.2 = bf16[64,1024]{1,0:T(8,128)(2,1)S(1)} collective-permute-done((bf16[64,1024]{1,0:T(8,128)(2,1)S(1)}, bf16[64,1024]{1,0:T(8,128)(2,1)S(1)}, u32[]{:S(2)}, u32[]{:S(2)}) %collective-permute-start.2) | collective-permute-done | bytes 131104 | tf_op jit(solution)/shard_map/ppermute | solution.py:221
  28.0 2.0 %collective-permute-done.13 = bf16[64,1024]{1,0:T(8,128)(2,1)S(1)} collective-permute-done((bf16[64,1024]{1,0:T(8,128)(2,1)S(1)}, bf16[64,1024]{1,0:T(8,128)(2,1)S(1)}, u32[]{:S(2)}, u32[]{:S(2)}) %collective-permute-start.13) | collective-permute-done | bytes 131104 | tf_op jit(solution)/shard_map/ppermute | solution.py:221
  30.0 4.6 %collective-permute-start.14 = (bf16[64,1024]{1,0:T(8,128)(2,1)S(1)}, bf16[64,1024]{1,0:T(8,128)(2,1)S(1)}, u32[]{:S(2)}, u32[]{:S(2)}) collective-permute-start(bf16[64,1024]{1,0:T(8,128)(2,1)S(1)} %add_convert_fusion), channel_id=1, source_target_pairs={{0,192},{16,208},{32,224},{48,240},{64,128},{80,144},{96,160},{112... | collective-permute-start | bytes 393224 | tf_op jit(solution)/shard_map/ppermute | solution.py:221
  34.7 2.8 %others.1.refs_4_ = bf16[1,4,64,8192]{3,2,1,0:T(8,128)(2,1)} custom-call(s32[1]{0:T(128)S(6)} %copy.14.ids.after_ref, f32[64,512]{1,0:T(8,128)S(1)} %get-tuple-element.48.after_ref, bf16[1,4,64,8192]{3,2,1,0:T(8,128)(2,1)} %inner_hbm.5), custom_call_target="tpu_custom_call" | custom-call | bytes 6291456 | tf_op jit(solution)/shard_map/others/pallas_call | solution.py:134
  37.6 4.9 %collective-permute-start.6 = (bf16[64,1024]{1,0:T(8,128)(2,1)S(1)}, bf16[64,1024]{1,0:T(8,128)(2,1)S(1)}, u32[]{:S(2)}, u32[]{:S(2)}) collective-permute-start(bf16[64,1024]{1,0:T(8,128)(2,1)S(1)} %add_convert_fusion.2), channel_id=1, source_target_pairs={{0,64},{16,80},{32,96},{48,112},{64,0},{80,16},{96,32},{112,48},{1... | collective-permute-start | bytes 393224 | tf_op jit(solution)/shard_map/ppermute | solution.py:221
  42.7 1.0 %collective-permute-start.17 = (bf16[64,1024]{1,0:T(8,128)(2,1)S(1)}, bf16[64,1024]{1,0:T(8,128)(2,1)S(1)}, u32[]{:S(2)}, u32[]{:S(2)}) collective-permute-start(bf16[64,1024]{1,0:T(8,128)(2,1)S(1)} %get-tuple-element.42.refs_0_), channel_id=1, source_target_pairs={{0,32},{16,48},{32,0},{48,16},{64,96},{80,112},{96,64},{112,80},{1... | collective-permute-start | bytes 393224 | tf_op jit(solution)/shard_map/ppermute | solution.py:221
  43.7 1.5 %collective-permute-start.16 = (bf16[64,1024]{1,0:T(8,128)(2,1)S(1)}, bf16[64,1024]{1,0:T(8,128)(2,1)S(1)}, u32[]{:S(2)}, u32[]{:S(2)}) collective-permute-start(bf16[64,1024]{1,0:T(8,128)(2,1)S(1)} %get-tuple-element.42.refs_0_), channel_id=1, source_target_pairs={{0,16},{16,32},{32,48},{48,0},{64,80},{80,96},{96,112},{112,64},{1... | collective-permute-start | bytes 393224 | tf_op jit(solution)/shard_map/ppermute | solution.py:221
  45.2 1.7 %collective-permute-start.15 = (bf16[64,1024]{1,0:T(8,128)(2,1)S(1)}, bf16[64,1024]{1,0:T(8,128)(2,1)S(1)}, u32[]{:S(2)}, u32[]{:S(2)}) collective-permute-start(bf16[64,1024]{1,0:T(8,128)(2,1)S(1)} %get-tuple-element.42.refs_0_), channel_id=1, source_target_pairs={{0,48},{16,0},{32,16},{48,32},{64,112},{80,64},{96,80},{112,96},{1... | collective-permute-start | bytes 393224 | tf_op jit(solution)/shard_map/ppermute | solution.py:221
  46.9 1.4 %collective-permute-done.6 = bf16[64,1024]{1,0:T(8,128)(2,1)S(1)} collective-permute-done((bf16[64,1024]{1,0:T(8,128)(2,1)S(1)}, bf16[64,1024]{1,0:T(8,128)(2,1)S(1)}, u32[]{:S(2)}, u32[]{:S(2)}) %collective-permute-start.6) | collective-permute-done | bytes 131104 | tf_op jit(solution)/shard_map/ppermute | solution.py:221
  48.4 0.8 %collective-permute-start.9 = (bf16[64,1024]{1,0:T(8,128)(2,1)S(1)}, bf16[64,1024]{1,0:T(8,128)(2,1)S(1)}, u32[]{:S(2)}, u32[]{:S(2)}) collective-permute-start(bf16[64,1024]{1,0:T(8,128)(2,1)S(1)} %get-tuple-element.40.refs_0_), channel_id=1, source_target_pairs={{0,32},{16,48},{32,0},{48,16},{64,96},{80,112},{96,64},{112,80},{1... | collective-permute-start | bytes 393224 | tf_op jit(solution)/shard_map/ppermute | solution.py:221
  49.2 1.4 %collective-permute-start.8 = (bf16[64,1024]{1,0:T(8,128)(2,1)S(1)}, bf16[64,1024]{1,0:T(8,128)(2,1)S(1)}, u32[]{:S(2)}, u32[]{:S(2)}) collective-permute-start(bf16[64,1024]{1,0:T(8,128)(2,1)S(1)} %get-tuple-element.40.refs_0_), channel_id=1, source_target_pairs={{0,16},{16,32},{32,48},{48,0},{64,80},{80,96},{96,112},{112,64},{1... | collective-permute-start | bytes 393224 | tf_op jit(solution)/shard_map/ppermute | solution.py:221
  50.7 1.8 %collective-permute-start.7 = (bf16[64,1024]{1,0:T(8,128)(2,1)S(1)}, bf16[64,1024]{1,0:T(8,128)(2,1)S(1)}, u32[]{:S(2)}, u32[]{:S(2)}) collective-permute-start(bf16[64,1024]{1,0:T(8,128)(2,1)S(1)} %get-tuple-element.40.refs_0_), channel_id=1, source_target_pairs={{0,48},{16,0},{32,16},{48,32},{64,112},{80,64},{96,80},{112,96},{1... | collective-permute-start | bytes 393224 | tf_op jit(solution)/shard_map/ppermute | solution.py:221
  52.5 0.8 %collective-permute-done.16.refs_2_ = bf16[64,1024]{1,0:T(8,128)(2,1)S(1)} collective-permute-done((bf16[64,1024]{1,0:T(8,128)(2,1)S(1)}, bf16[64,1024]{1,0:T(8,128)(2,1)S(1)}, u32[]{:S(2)}, u32[]{:S(2)}) %collective-permute-start.16) | collective-permute-done | bytes 131104 | tf_op jit(solution)/shard_map/ppermute | solution.py:221
  53.2 1.0 %blend0.1 = (bf16[64,8192]{1,0:T(8,128)(2,1)}, bf16[1,4,64,8192]{3,2,1,0:T(8,128)(2,1)}) custom-call(s32[1]{0:T(128)S(6)} %copy.14.ids.after_ref, bf16[64,4096]{1,0:T(8,128)(2,1)S(1)} %get-tuple-element.28.chosen, bf16[64,1024]{1,0:T(8,128)(2,1)S(1)} %get-tuple-element.42.refs_0_, ...), custom_call_target="tpu_custom_call", output_to_operand_aliasing={{1}: (6, {})} | custom-call | flops 1048576 | bytes 2097152 | tf_op jit(solution)/shard_map/blend0/pallas_call | solution.py:192
  55.1 1.3 %collective-permute-done.8.refs_2_ = bf16[64,1024]{1,0:T(8,128)(2,1)S(1)} collective-permute-done((bf16[64,1024]{1,0:T(8,128)(2,1)S(1)}, bf16[64,1024]{1,0:T(8,128)(2,1)S(1)}, u32[]{:S(2)}, u32[]{:S(2)}) %collective-permute-start.8) | collective-permute-done | bytes 131104 | tf_op jit(solution)/shard_map/ppermute | solution.py:221
  56.4 1.0 %blend1.1 = (bf16[64,8192]{1,0:T(8,128)(2,1)}, bf16[1,4,64,8192]{3,2,1,0:T(8,128)(2,1)}) custom-call(s32[1]{0:T(128)S(6)} %copy.14.ids.after_ref, bf16[64,4096]{1,0:T(8,128)(2,1)S(1)} %get-tuple-element.21.chosen, bf16[64,1024]{1,0:T(8,128)(2,1)S(1)} %get-tuple-element.40.refs_0_, ...), custom_call_target="tpu_custom_call", output_to_operand_aliasing={{0}: (6, {}), {1}: (7, {})} | custom-call | flops 1048576 | bytes 2097152 | tf_op jit(solution)/shard_map/blend1/pallas_call | solution.py:192
  (29 shorter events, 3.5 us)
Async XLA Ops:
  0.6 12.3 %copy-start = (f32[64,512]{1,0:T(8,128)S(1)}, f32[64,512]{1,0:T(8,128)}, u32[]{:S(2)}) copy-start(f32[64,512]{1,0:T(8,128)} %param.7) | copy-start | bytes 393220
  0.6 12.3 %collective-permute-start = (f32[64,512]{1,0:T(8,128)}, f32[64,512]{1,0:T(8,128)S(1)}, u32[]{:S(2)}, u32[]{:S(2)}) collective-permute-start(f32[64,512]{1,0:T(8,128)} %param.7), channel_id=1, source_target_pairs={{0,64},{16,80},{32,96},{48,112},{64,0},{80,16},{96,32},{112,48},{1... | collective-permute-start | bytes 393224 | tf_op jit(solution)/shard_map/ppermute | solution.py:221
  6.4 13.1 %collective-permute-start.10 = (bf16[64,1024]{1,0:T(8,128)(2,1)S(1)}, bf16[64,1024]{1,0:T(8,128)(2,1)S(1)}, u32[]{:S(2)}, u32[]{:S(2)}) collective-permute-start(bf16[64,1024]{1,0:T(8,128)(2,1)S(1)} %get-tuple-element.31), channel_id=1, source_target_pairs={{0,32},{16,48},{32,0},{48,16},{64,96},{80,112},{96,64},{112,80},{1... | collective-permute-start | bytes 393224 | tf_op jit(solution)/shard_map/ppermute | solution.py:221
  9.7 10.6 %collective-permute-start.11 = (bf16[64,1024]{1,0:T(8,128)(2,1)S(1)}, bf16[64,1024]{1,0:T(8,128)(2,1)S(1)}, u32[]{:S(2)}, u32[]{:S(2)}) collective-permute-start(bf16[64,1024]{1,0:T(8,128)(2,1)S(1)} %get-tuple-element.32), channel_id=1, source_target_pairs={{0,16},{16,32},{32,48},{48,0},{64,80},{80,96},{96,112},{112,64},{1... | collective-permute-start | bytes 393224 | tf_op jit(solution)/shard_map/ppermute | solution.py:221
  10.4 12.4 %collective-permute-start.12 = (bf16[64,1024]{1,0:T(8,128)(2,1)S(1)}, bf16[64,1024]{1,0:T(8,128)(2,1)S(1)}, u32[]{:S(2)}, u32[]{:S(2)}) collective-permute-start(bf16[64,1024]{1,0:T(8,128)(2,1)S(1)} %get-tuple-element.33), channel_id=1, source_target_pairs={{0,48},{16,0},{32,16},{48,32},{64,112},{80,64},{96,80},{112,96},{1... | collective-permute-start | bytes 393224 | tf_op jit(solution)/shard_map/ppermute | solution.py:221
  13.0 21.7 %collective-permute-start.5 = (f32[64,1024]{1,0:T(8,128)S(1)}, f32[64,1024]{1,0:T(8,128)S(1)}, u32[]{:S(2)}, u32[]{:S(2)}) collective-permute-start(f32[64,1024]{1,0:T(8,128)S(1)} %pad_maximum_fusion.after_ref), channel_id=1, source_target_pairs={{0,192},{16,208},{32,224},{48,240},{64,128},{80,144},{96,160},{112... | collective-permute-start | bytes 786440 | tf_op jit(solution)/shard_map/ppermute | solution.py:221
  19.3 6.9 %collective-permute-start.1 = (bf16[64,1024]{1,0:T(8,128)(2,1)S(1)}, bf16[64,1024]{1,0:T(8,128)(2,1)S(1)}, u32[]{:S(2)}, u32[]{:S(2)}) collective-permute-start(bf16[64,1024]{1,0:T(8,128)(2,1)S(1)} %get-tuple-element.24), channel_id=1, source_target_pairs={{0,32},{16,48},{32,0},{48,16},{64,96},{80,112},{96,64},{112,80},{1... | collective-permute-start | bytes 393224 | tf_op jit(solution)/shard_map/ppermute | solution.py:221
  19.5 8.0 %collective-permute-start.2 = (bf16[64,1024]{1,0:T(8,128)(2,1)S(1)}, bf16[64,1024]{1,0:T(8,128)(2,1)S(1)}, u32[]{:S(2)}, u32[]{:S(2)}) collective-permute-start(bf16[64,1024]{1,0:T(8,128)(2,1)S(1)} %get-tuple-element.25), channel_id=1, source_target_pairs={{0,16},{16,32},{32,48},{48,0},{64,80},{80,96},{96,112},{112,64},{1... | collective-permute-start | bytes 393224 | tf_op jit(solution)/shard_map/ppermute | solution.py:221
  20.3 7.3 %collective-permute-start.3 = (bf16[64,1024]{1,0:T(8,128)(2,1)S(1)}, bf16[64,1024]{1,0:T(8,128)(2,1)S(1)}, u32[]{:S(2)}, u32[]{:S(2)}) collective-permute-start(bf16[64,1024]{1,0:T(8,128)(2,1)S(1)} %get-tuple-element.26), channel_id=1, source_target_pairs={{0,48},{16,0},{32,16},{48,32},{64,112},{80,64},{96,80},{112,96},{1... | collective-permute-start | bytes 393224 | tf_op jit(solution)/shard_map/ppermute | solution.py:221
  22.9 7.1 %collective-permute-start.13 = (bf16[64,1024]{1,0:T(8,128)(2,1)S(1)}, bf16[64,1024]{1,0:T(8,128)(2,1)S(1)}, u32[]{:S(2)}, u32[]{:S(2)}) collective-permute-start(bf16[64,1024]{1,0:T(8,128)(2,1)S(1)} %add_convert_fusion.1), channel_id=1, source_target_pairs={{0,64},{16,80},{32,96},{48,112},{64,0},{80,16},{96,32},{112,48},{1... | collective-permute-start | bytes 393224 | tf_op jit(solution)/shard_map/ppermute | solution.py:221
  27.6 9.9 %collective-permute-start.4 = (bf16[64,1024]{1,0:T(8,128)(2,1)S(1)}, bf16[64,1024]{1,0:T(8,128)(2,1)S(1)}, u32[]{:S(2)}, u32[]{:S(2)}) collective-permute-start(bf16[64,1024]{1,0:T(8,128)(2,1)S(1)} %add_convert_fusion.3), channel_id=1, source_target_pairs={{0,192},{16,208},{32,224},{48,240},{64,128},{80,144},{96,160},{112... | collective-permute-start | bytes 393224 | tf_op jit(solution)/shard_map/ppermute | solution.py:221
  30.0 12.5 %collective-permute-start.14 = (bf16[64,1024]{1,0:T(8,128)(2,1)S(1)}, bf16[64,1024]{1,0:T(8,128)(2,1)S(1)}, u32[]{:S(2)}, u32[]{:S(2)}) collective-permute-start(bf16[64,1024]{1,0:T(8,128)(2,1)S(1)} %add_convert_fusion), channel_id=1, source_target_pairs={{0,192},{16,208},{32,224},{48,240},{64,128},{80,144},{96,160},{112... | collective-permute-start | bytes 393224 | tf_op jit(solution)/shard_map/ppermute | solution.py:221
  37.6 10.7 %collective-permute-start.6 = (bf16[64,1024]{1,0:T(8,128)(2,1)S(1)}, bf16[64,1024]{1,0:T(8,128)(2,1)S(1)}, u32[]{:S(2)}, u32[]{:S(2)}) collective-permute-start(bf16[64,1024]{1,0:T(8,128)(2,1)S(1)} %add_convert_fusion.2), channel_id=1, source_target_pairs={{0,64},{16,80},{32,96},{48,112},{64,0},{80,16},{96,32},{112,48},{1... | collective-permute-start | bytes 393224 | tf_op jit(solution)/shard_map/ppermute | solution.py:221
  42.7 8.0 %collective-permute-start.17 = (bf16[64,1024]{1,0:T(8,128)(2,1)S(1)}, bf16[64,1024]{1,0:T(8,128)(2,1)S(1)}, u32[]{:S(2)}, u32[]{:S(2)}) collective-permute-start(bf16[64,1024]{1,0:T(8,128)(2,1)S(1)} %get-tuple-element.42.refs_0_), channel_id=1, source_target_pairs={{0,32},{16,48},{32,0},{48,16},{64,96},{80,112},{96,64},{112,80},{1... | collective-permute-start | bytes 393224 | tf_op jit(solution)/shard_map/ppermute | solution.py:221
  43.7 9.5 %collective-permute-start.16 = (bf16[64,1024]{1,0:T(8,128)(2,1)S(1)}, bf16[64,1024]{1,0:T(8,128)(2,1)S(1)}, u32[]{:S(2)}, u32[]{:S(2)}) collective-permute-start(bf16[64,1024]{1,0:T(8,128)(2,1)S(1)} %get-tuple-element.42.refs_0_), channel_id=1, source_target_pairs={{0,16},{16,32},{32,48},{48,0},{64,80},{80,96},{96,112},{112,64},{1... | collective-permute-start | bytes 393224 | tf_op jit(solution)/shard_map/ppermute | solution.py:221
  45.2 8.0 %collective-permute-start.15 = (bf16[64,1024]{1,0:T(8,128)(2,1)S(1)}, bf16[64,1024]{1,0:T(8,128)(2,1)S(1)}, u32[]{:S(2)}, u32[]{:S(2)}) collective-permute-start(bf16[64,1024]{1,0:T(8,128)(2,1)S(1)} %get-tuple-element.42.refs_0_), channel_id=1, source_target_pairs={{0,48},{16,0},{32,16},{48,32},{64,112},{80,64},{96,80},{112,96},{1... | collective-permute-start | bytes 393224 | tf_op jit(solution)/shard_map/ppermute | solution.py:221
  48.4 6.7 %collective-permute-start.9 = (bf16[64,1024]{1,0:T(8,128)(2,1)S(1)}, bf16[64,1024]{1,0:T(8,128)(2,1)S(1)}, u32[]{:S(2)}, u32[]{:S(2)}) collective-permute-start(bf16[64,1024]{1,0:T(8,128)(2,1)S(1)} %get-tuple-element.40.refs_0_), channel_id=1, source_target_pairs={{0,32},{16,48},{32,0},{48,16},{64,96},{80,112},{96,64},{112,80},{1... | collective-permute-start | bytes 393224 | tf_op jit(solution)/shard_map/ppermute | solution.py:221
  49.2 7.2 %collective-permute-start.8 = (bf16[64,1024]{1,0:T(8,128)(2,1)S(1)}, bf16[64,1024]{1,0:T(8,128)(2,1)S(1)}, u32[]{:S(2)}, u32[]{:S(2)}) collective-permute-start(bf16[64,1024]{1,0:T(8,128)(2,1)S(1)} %get-tuple-element.40.refs_0_), channel_id=1, source_target_pairs={{0,16},{16,32},{32,48},{48,0},{64,80},{80,96},{96,112},{112,64},{1... | collective-permute-start | bytes 393224 | tf_op jit(solution)/shard_map/ppermute | solution.py:221
  50.7 5.7 %collective-permute-start.7 = (bf16[64,1024]{1,0:T(8,128)(2,1)S(1)}, bf16[64,1024]{1,0:T(8,128)(2,1)S(1)}, u32[]{:S(2)}, u32[]{:S(2)}) collective-permute-start(bf16[64,1024]{1,0:T(8,128)(2,1)S(1)} %get-tuple-element.40.refs_0_), channel_id=1, source_target_pairs={{0,48},{16,0},{32,16},{48,32},{64,112},{80,64},{96,80},{112,96},{1... | collective-permute-start | bytes 393224 | tf_op jit(solution)/shard_map/ppermute | solution.py:221

commit v4 on v3

--- a/solution.py
+++ b/solution.py
@@ -239,7 +239,7 @@
         snaps.append(snap)
         kept.append(chosen)
     for c in range(CHUNKS):
-        got = [sent[c][0]] + [send(sent[c][k], y_shift(k)) for k in (2, 1, 3)]
+        got = [sent[c][0]] + [send(sent[c][k], y_shift(k)) for k in (1, 2, 3)]
         parts.append(sum(g.astype(f32) for g in got).astype(bf16))
     others = others_copied(ids, moments[0], inner)
     grads, news = [], []

time: 58.4 us -> 56.7 us (0.971)
  waiting for transfers between devices: 6.84 us -> 4.93 us
    ppermute x18, waiting for transfers between devices: 6.84 us -> 4.93 us  [send(): return lax.ppermute(x, 'replica', perm)]
  transfers between devices with their start and end apart: 18 -> 18, of which waited for: 6 -> 5; matrix products, arithmetic and copies ran while one was open for 2% -> 2% of each run, Pallas kernels for 13% -> 13%
where the time goes in v4:
time: 56.7 us; the launch traced here: 56 us
  starting transfers between devices  40 us (71%)
  Pallas kernels  8.4 us (15%)
  waiting for transfers between devices  4.93 us (9%)
  between operations  1.39 us (2%)
  other arithmetic  1.29 us (2%)
    ppermute x18, starting transfers between devices, send(): return lax.ppermute(x, 'replica', perm)  40 us
    ppermute x18, waiting for transfers between devices, send(): return lax.ppermute(x, 'replica', perm)  4.93 us
    pallas_call x2, Pallas kernels, rounded_blocks(): pl.pallas_call(functools.partial(round_kernel, chunk, share), out_shape=[...  3.51 us
    pallas_call x1, Pallas kernels, others_copied(): pl.pallas_call(copy_kernel, out_shape=jax.ShapeDtypeStruct(inner.shape, i...  2.81 us
    pallas_call x2, Pallas kernels, blended(): pl.pallas_call(functools.partial(blend_kernel, chunk, share), out_shape=[...  2.08 us
  transfers between devices with their start and end apart: 18, of which 5 were waited for; matrix products, arithmetic and copies ran while one was open for 2% of the time, Pallas kernels for 13%

profile of v4, /device:TPU:2, one launch (start us, length us, event | category | flops | bytes accessed | tf_op | source)
XLA Modules:
  0.0 56.0 jit_solution(1565976992252024604)
XLA Ops:
  0.6 3.4 %collective-permute-start = (f32[64,512]{1,0:T(8,128)}, f32[64,512]{1,0:T(8,128)S(1)}, u32[]{:S(2)}, u32[]{:S(2)}) collective-permute-start(f32[64,512]{1,0:T(8,128)} %param.7), channel_id=1, source_target_pairs={{0,64},{16,80},{32,96},{48,112},{64,0},{80,16},{96,32},{112,48},{1... | collective-permute-start | bytes 393224 | tf_op jit(solution)/shard_map/ppermute | solution.py:221
  4.6 1.8 %round0.1 = (bf16[64,1024]{1,0:T(8,128)(2,1)S(1)}, bf16[64,1024]{1,0:T(8,128)(2,1)S(1)}, bf16[64,1024]{1,0:T(8,128)(2,1)S(1)}, bf16[64,1024]{1,0:T(8,128)(2,1)S(...) custom-call(s32[1]{0:T(128)S(6)} %copy.14.ids.after_ref, s32[1]{0:T(128)S(6)} %copy.14.ids.after_ref, ...), custom_call_target="tpu_custom_call" | custom-call | flops 3145728 | bytes 2621440 | tf_op jit(solution)/shard_map/round0/pallas_call | solution.py:86
  6.4 1.7 %collective-permute-start.10 = (bf16[64,1024]{1,0:T(8,128)(2,1)S(1)}, bf16[64,1024]{1,0:T(8,128)(2,1)S(1)}, u32[]{:S(2)}, u32[]{:S(2)}) collective-permute-start(bf16[64,1024]{1,0:T(8,128)(2,1)S(1)} %get-tuple-element.31), channel_id=1, source_target_pairs={{0,16},{16,32},{32,48},{48,0},{64,80},{80,96},{96,112},{112,64},{1... | collective-permute-start | bytes 393224 | tf_op jit(solution)/shard_map/ppermute | solution.py:221
  8.1 2.9 %collective-permute-start.11 = (bf16[64,1024]{1,0:T(8,128)(2,1)S(1)}, bf16[64,1024]{1,0:T(8,128)(2,1)S(1)}, u32[]{:S(2)}, u32[]{:S(2)}) collective-permute-start(bf16[64,1024]{1,0:T(8,128)(2,1)S(1)} %get-tuple-element.32), channel_id=1, source_target_pairs={{0,32},{16,48},{32,0},{48,16},{64,96},{80,112},{96,64},{112,80},{1... | collective-permute-start | bytes 393224 | tf_op jit(solution)/shard_map/ppermute | solution.py:221
  11.0 1.3 %collective-permute-start.12 = (bf16[64,1024]{1,0:T(8,128)(2,1)S(1)}, bf16[64,1024]{1,0:T(8,128)(2,1)S(1)}, u32[]{:S(2)}, u32[]{:S(2)}) collective-permute-start(bf16[64,1024]{1,0:T(8,128)(2,1)S(1)} %get-tuple-element.33), channel_id=1, source_target_pairs={{0,48},{16,0},{32,16},{48,32},{64,112},{80,64},{96,80},{112,96},{1... | collective-permute-start | bytes 393224 | tf_op jit(solution)/shard_map/ppermute | solution.py:221
  12.4 4.6 %collective-permute-start.5 = (f32[64,1024]{1,0:T(8,128)S(1)}, f32[64,1024]{1,0:T(8,128)S(1)}, u32[]{:S(2)}, u32[]{:S(2)}) collective-permute-start(f32[64,1024]{1,0:T(8,128)S(1)} %pad_maximum_fusion.after_ref), channel_id=1, source_target_pairs={{0,192},{16,208},{32,224},{48,240},{64,128},{80,144},{96,160},{112... | collective-permute-start | bytes 786440 | tf_op jit(solution)/shard_map/ppermute | solution.py:221
  16.9 1.8 %round1.1 = (bf16[64,1024]{1,0:T(8,128)(2,1)S(1)}, bf16[64,1024]{1,0:T(8,128)(2,1)S(1)}, bf16[64,1024]{1,0:T(8,128)(2,1)S(1)}, bf16[64,1024]{1,0:T(8,128)(2,1)S(...) custom-call(s32[1]{0:T(128)S(6)} %copy.14.ids.after_ref, f32[64,1024]{1,0:T(8,128)S(1)} %pad_maximum_fusion.after_ref, ...), custom_call_target="tpu_custom_call" | custom-call | flops 3145728 | bytes 2621440 | tf_op jit(solution)/shard_map/round1/pallas_call | solution.py:86
  18.7 0.8 %collective-permute-start.1 = (bf16[64,1024]{1,0:T(8,128)(2,1)S(1)}, bf16[64,1024]{1,0:T(8,128)(2,1)S(1)}, u32[]{:S(2)}, u32[]{:S(2)}) collective-permute-start(bf16[64,1024]{1,0:T(8,128)(2,1)S(1)} %get-tuple-element.24), channel_id=1, source_target_pairs={{0,16},{16,32},{32,48},{48,0},{64,80},{80,96},{96,112},{112,64},{1... | collective-permute-start | bytes 393224 | tf_op jit(solution)/shard_map/ppermute | solution.py:221
  19.5 1.4 %collective-permute-start.2 = (bf16[64,1024]{1,0:T(8,128)(2,1)S(1)}, bf16[64,1024]{1,0:T(8,128)(2,1)S(1)}, u32[]{:S(2)}, u32[]{:S(2)}) collective-permute-start(bf16[64,1024]{1,0:T(8,128)(2,1)S(1)} %get-tuple-element.25), channel_id=1, source_target_pairs={{0,32},{16,48},{32,0},{48,16},{64,96},{80,112},{96,64},{112,80},{1... | collective-permute-start | bytes 393224 | tf_op jit(solution)/shard_map/ppermute | solution.py:221
  20.8 1.4 %collective-permute-start.3 = (bf16[64,1024]{1,0:T(8,128)(2,1)S(1)}, bf16[64,1024]{1,0:T(8,128)(2,1)S(1)}, u32[]{:S(2)}, u32[]{:S(2)}) collective-permute-start(bf16[64,1024]{1,0:T(8,128)(2,1)S(1)} %get-tuple-element.26), channel_id=1, source_target_pairs={{0,48},{16,0},{32,16},{48,32},{64,112},{80,64},{96,80},{112,96},{1... | collective-permute-start | bytes 393224 | tf_op jit(solution)/shard_map/ppermute | solution.py:221
  22.3 3.3 %collective-permute-start.13 = (bf16[64,1024]{1,0:T(8,128)(2,1)S(1)}, bf16[64,1024]{1,0:T(8,128)(2,1)S(1)}, u32[]{:S(2)}, u32[]{:S(2)}) collective-permute-start(bf16[64,1024]{1,0:T(8,128)(2,1)S(1)} %add_convert_fusion.1), channel_id=1, source_target_pairs={{0,64},{16,80},{32,96},{48,112},{64,0},{80,16},{96,32},{112,48},{1... | collective-permute-start | bytes 393224 | tf_op jit(solution)/shard_map/ppermute | solution.py:221
  25.6 1.2 %collective-permute-done.1 = bf16[64,1024]{1,0:T(8,128)(2,1)S(1)} collective-permute-done((bf16[64,1024]{1,0:T(8,128)(2,1)S(1)}, bf16[64,1024]{1,0:T(8,128)(2,1)S(1)}, u32[]{:S(2)}, u32[]{:S(2)}) %collective-permute-start.1) | collective-permute-done | bytes 131104 | tf_op jit(solution)/shard_map/ppermute | solution.py:221
  27.7 1.6 %collective-permute-done.13 = bf16[64,1024]{1,0:T(8,128)(2,1)S(1)} collective-permute-done((bf16[64,1024]{1,0:T(8,128)(2,1)S(1)}, bf16[64,1024]{1,0:T(8,128)(2,1)S(1)}, u32[]{:S(2)}, u32[]{:S(2)}) %collective-permute-start.13) | collective-permute-done | bytes 131104 | tf_op jit(solution)/shard_map/ppermute | solution.py:221
  29.4 4.3 %collective-permute-start.14 = (bf16[64,1024]{1,0:T(8,128)(2,1)S(1)}, bf16[64,1024]{1,0:T(8,128)(2,1)S(1)}, u32[]{:S(2)}, u32[]{:S(2)}) collective-permute-start(bf16[64,1024]{1,0:T(8,128)(2,1)S(1)} %add_convert_fusion), channel_id=1, source_target_pairs={{0,192},{16,208},{32,224},{48,240},{64,128},{80,144},{96,160},{112... | collective-permute-start | bytes 393224 | tf_op jit(solution)/shard_map/ppermute | solution.py:221
  33.7 2.8 %others.1.refs_4_ = bf16[1,4,64,8192]{3,2,1,0:T(8,128)(2,1)} custom-call(s32[1]{0:T(128)S(6)} %copy.14.ids.after_ref, f32[64,512]{1,0:T(8,128)S(1)} %get-tuple-element.48.after_ref, bf16[1,4,64,8192]{3,2,1,0:T(8,128)(2,1)} %inner_hbm.5), custom_call_target="tpu_custom_call" | custom-call | bytes 6291456 | tf_op jit(solution)/shard_map/others/pallas_call | solution.py:134
  36.6 4.9 %collective-permute-start.6 = (bf16[64,1024]{1,0:T(8,128)(2,1)S(1)}, bf16[64,1024]{1,0:T(8,128)(2,1)S(1)}, u32[]{:S(2)}, u32[]{:S(2)}) collective-permute-start(bf16[64,1024]{1,0:T(8,128)(2,1)S(1)} %add_convert_fusion.2), channel_id=1, source_target_pairs={{0,64},{16,80},{32,96},{48,112},{64,0},{80,16},{96,32},{112,48},{1... | collective-permute-start | bytes 393224 | tf_op jit(solution)/shard_map/ppermute | solution.py:221
  41.6 1.6 %collective-permute-start.17 = (bf16[64,1024]{1,0:T(8,128)(2,1)S(1)}, bf16[64,1024]{1,0:T(8,128)(2,1)S(1)}, u32[]{:S(2)}, u32[]{:S(2)}) collective-permute-start(bf16[64,1024]{1,0:T(8,128)(2,1)S(1)} %get-tuple-element.42.refs_0_), channel_id=1, source_target_pairs={{0,32},{16,48},{32,0},{48,16},{64,96},{80,112},{96,64},{112,80},{1... | collective-permute-start | bytes 393224 | tf_op jit(solution)/shard_map/ppermute | solution.py:221
  43.2 2.7 %collective-permute-start.16 = (bf16[64,1024]{1,0:T(8,128)(2,1)S(1)}, bf16[64,1024]{1,0:T(8,128)(2,1)S(1)}, u32[]{:S(2)}, u32[]{:S(2)}) collective-permute-start(bf16[64,1024]{1,0:T(8,128)(2,1)S(1)} %get-tuple-element.42.refs_0_), channel_id=1, source_target_pairs={{0,16},{16,32},{32,48},{48,0},{64,80},{80,96},{96,112},{112,64},{1... | collective-permute-start | bytes 393224 | tf_op jit(solution)/shard_map/ppermute | solution.py:221
  46.6 2.3 %collective-permute-start.9 = (bf16[64,1024]{1,0:T(8,128)(2,1)S(1)}, bf16[64,1024]{1,0:T(8,128)(2,1)S(1)}, u32[]{:S(2)}, u32[]{:S(2)}) collective-permute-start(bf16[64,1024]{1,0:T(8,128)(2,1)S(1)} %get-tuple-element.40.refs_0_), channel_id=1, source_target_pairs={{0,32},{16,48},{32,0},{48,16},{64,96},{80,112},{96,64},{112,80},{1... | collective-permute-start | bytes 393224 | tf_op jit(solution)/shard_map/ppermute | solution.py:221
  49.5 2.5 %collective-permute-start.7 = (bf16[64,1024]{1,0:T(8,128)(2,1)S(1)}, bf16[64,1024]{1,0:T(8,128)(2,1)S(1)}, u32[]{:S(2)}, u32[]{:S(2)}) collective-permute-start(bf16[64,1024]{1,0:T(8,128)(2,1)S(1)} %get-tuple-element.40.refs_0_), channel_id=1, source_target_pairs={{0,48},{16,0},{32,16},{48,32},{64,112},{80,64},{96,80},{112,96},{1... | collective-permute-start | bytes 393224 | tf_op jit(solution)/shard_map/ppermute | solution.py:221
  52.1 1.0 %blend0.1 = (bf16[64,8192]{1,0:T(8,128)(2,1)}, bf16[1,4,64,8192]{3,2,1,0:T(8,128)(2,1)}) custom-call(s32[1]{0:T(128)S(6)} %copy.14.ids.after_ref, bf16[64,4096]{1,0:T(8,128)(2,1)S(1)} %get-tuple-element.28.chosen, bf16[64,1024]{1,0:T(8,128)(2,1)S(1)} %get-tuple-element.42.refs_0_, ...), custom_call_target="tpu_custom_call", output_to_operand_aliasing={{1}: (6, {})} | custom-call | flops 1048576 | bytes 2097152 | tf_op jit(solution)/shard_map/blend0/pallas_call | solution.py:192
  53.2 0.7 %fusion.20 = f32[64,512]{1,0:T(8,128)} fusion(f32[64,1024]{1,0:T(8,128)S(1)} %get-tuple-element.41, f32[64,1024]{1,0:T(8,128)S(1)} %get-tuple-element.39, f32[64,512]{1,0:T(8,128)S(1)} %copy-done, pred[]{:T(512)S(6)} %eq.19, pred[]{:T(512)S(6)} %eq.18, pred[]{:T(512)S(6)} %eq.17), kind=kLoop, calls=%fused_computation.32 | loop fusion | flops 163840 | bytes 786435 | tf_op jit(solution)/shard_map/add | solution.py:269
  53.9 1.1 %collective-permute-done.8.refs_2_ = bf16[64,1024]{1,0:T(8,128)(2,1)S(1)} collective-permute-done((bf16[64,1024]{1,0:T(8,128)(2,1)S(1)}, bf16[64,1024]{1,0:T(8,128)(2,1)S(1)}, u32[]{:S(2)}, u32[]{:S(2)}) %collective-permute-start.8) | collective-permute-done | bytes 131104 | tf_op jit(solution)/shard_map/ppermute | solution.py:221
  55.0 1.0 %blend1.1 = (bf16[64,8192]{1,0:T(8,128)(2,1)}, bf16[1,4,64,8192]{3,2,1,0:T(8,128)(2,1)}) custom-call(s32[1]{0:T(128)S(6)} %copy.14.ids.after_ref, bf16[64,4096]{1,0:T(8,128)(2,1)S(1)} %get-tuple-element.21.chosen, bf16[64,1024]{1,0:T(8,128)(2,1)S(1)} %get-tuple-element.40.refs_0_, ...), custom_call_target="tpu_custom_call", output_to_operand_aliasing={{0}: (6, {}), {1}: (7, {})} | custom-call | flops 1048576 | bytes 2097152 | tf_op jit(solution)/shard_map/blend1/pallas_call | solution.py:192
  (29 shorter events, 2.7 us)
Async XLA Ops:
  0.6 11.7 %copy-start = (f32[64,512]{1,0:T(8,128)S(1)}, f32[64,512]{1,0:T(8,128)}, u32[]{:S(2)}) copy-start(f32[64,512]{1,0:T(8,128)} %param.7) | copy-start | bytes 393220
  0.6 11.7 %collective-permute-start = (f32[64,512]{1,0:T(8,128)}, f32[64,512]{1,0:T(8,128)S(1)}, u32[]{:S(2)}, u32[]{:S(2)}) collective-permute-start(f32[64,512]{1,0:T(8,128)} %param.7), channel_id=1, source_target_pairs={{0,64},{16,80},{32,96},{48,112},{64,0},{80,16},{96,32},{112,48},{1... | collective-permute-start | bytes 393224 | tf_op jit(solution)/shard_map/ppermute | solution.py:221
  6.4 13.1 %collective-permute-start.10 = (bf16[64,1024]{1,0:T(8,128)(2,1)S(1)}, bf16[64,1024]{1,0:T(8,128)(2,1)S(1)}, u32[]{:S(2)}, u32[]{:S(2)}) collective-permute-start(bf16[64,1024]{1,0:T(8,128)(2,1)S(1)} %get-tuple-element.31), channel_id=1, source_target_pairs={{0,16},{16,32},{32,48},{48,0},{64,80},{80,96},{96,112},{112,64},{1... | collective-permute-start | bytes 393224 | tf_op jit(solution)/shard_map/ppermute | solution.py:221
  8.1 12.8 %collective-permute-start.11 = (bf16[64,1024]{1,0:T(8,128)(2,1)S(1)}, bf16[64,1024]{1,0:T(8,128)(2,1)S(1)}, u32[]{:S(2)}, u32[]{:S(2)}) collective-permute-start(bf16[64,1024]{1,0:T(8,128)(2,1)S(1)} %get-tuple-element.32), channel_id=1, source_target_pairs={{0,32},{16,48},{32,0},{48,16},{64,96},{80,112},{96,64},{112,80},{1... | collective-permute-start | bytes 393224 | tf_op jit(solution)/shard_map/ppermute | solution.py:221
  11.0 11.3 %collective-permute-start.12 = (bf16[64,1024]{1,0:T(8,128)(2,1)S(1)}, bf16[64,1024]{1,0:T(8,128)(2,1)S(1)}, u32[]{:S(2)}, u32[]{:S(2)}) collective-permute-start(bf16[64,1024]{1,0:T(8,128)(2,1)S(1)} %get-tuple-element.33), channel_id=1, source_target_pairs={{0,48},{16,0},{32,16},{48,32},{64,112},{80,64},{96,80},{112,96},{1... | collective-permute-start | bytes 393224 | tf_op jit(solution)/shard_map/ppermute | solution.py:221
  12.4 21.3 %collective-permute-start.5 = (f32[64,1024]{1,0:T(8,128)S(1)}, f32[64,1024]{1,0:T(8,128)S(1)}, u32[]{:S(2)}, u32[]{:S(2)}) collective-permute-start(f32[64,1024]{1,0:T(8,128)S(1)} %pad_maximum_fusion.after_ref), channel_id=1, source_target_pairs={{0,192},{16,208},{32,224},{48,240},{64,128},{80,144},{96,160},{112... | collective-permute-start | bytes 786440 | tf_op jit(solution)/shard_map/ppermute | solution.py:221
  18.7 8.1 %collective-permute-start.1 = (bf16[64,1024]{1,0:T(8,128)(2,1)S(1)}, bf16[64,1024]{1,0:T(8,128)(2,1)S(1)}, u32[]{:S(2)}, u32[]{:S(2)}) collective-permute-start(bf16[64,1024]{1,0:T(8,128)(2,1)S(1)} %get-tuple-element.24), channel_id=1, source_target_pairs={{0,16},{16,32},{32,48},{48,0},{64,80},{80,96},{96,112},{112,64},{1... | collective-permute-start | bytes 393224 | tf_op jit(solution)/shard_map/ppermute | solution.py:221
  19.5 7.4 %collective-permute-start.2 = (bf16[64,1024]{1,0:T(8,128)(2,1)S(1)}, bf16[64,1024]{1,0:T(8,128)(2,1)S(1)}, u32[]{:S(2)}, u32[]{:S(2)}) collective-permute-start(bf16[64,1024]{1,0:T(8,128)(2,1)S(1)} %get-tuple-element.25), channel_id=1, source_target_pairs={{0,32},{16,48},{32,0},{48,16},{64,96},{80,112},{96,64},{112,80},{1... | collective-permute-start | bytes 393224 | tf_op jit(solution)/shard_map/ppermute | solution.py:221
  20.8 6.4 %collective-permute-start.3 = (bf16[64,1024]{1,0:T(8,128)(2,1)S(1)}, bf16[64,1024]{1,0:T(8,128)(2,1)S(1)}, u32[]{:S(2)}, u32[]{:S(2)}) collective-permute-start(bf16[64,1024]{1,0:T(8,128)(2,1)S(1)} %get-tuple-element.26), channel_id=1, source_target_pairs={{0,48},{16,0},{32,16},{48,32},{64,112},{80,64},{96,80},{112,96},{1... | collective-permute-start | bytes 393224 | tf_op jit(solution)/shard_map/ppermute | solution.py:221
  22.3 7.0 %collective-permute-start.13 = (bf16[64,1024]{1,0:T(8,128)(2,1)S(1)}, bf16[64,1024]{1,0:T(8,128)(2,1)S(1)}, u32[]{:S(2)}, u32[]{:S(2)}) collective-permute-start(bf16[64,1024]{1,0:T(8,128)(2,1)S(1)} %add_convert_fusion.1), channel_id=1, source_target_pairs={{0,64},{16,80},{32,96},{48,112},{64,0},{80,16},{96,32},{112,48},{1... | collective-permute-start | bytes 393224 | tf_op jit(solution)/shard_map/ppermute | solution.py:221
  27.3 9.2 %collective-permute-start.4 = (bf16[64,1024]{1,0:T(8,128)(2,1)S(1)}, bf16[64,1024]{1,0:T(8,128)(2,1)S(1)}, u32[]{:S(2)}, u32[]{:S(2)}) collective-permute-start(bf16[64,1024]{1,0:T(8,128)(2,1)S(1)} %add_convert_fusion.3), channel_id=1, source_target_pairs={{0,192},{16,208},{32,224},{48,240},{64,128},{80,144},{96,160},{112... | collective-permute-start | bytes 393224 | tf_op jit(solution)/shard_map/ppermute | solution.py:221
  29.4 12.1 %collective-permute-start.14 = (bf16[64,1024]{1,0:T(8,128)(2,1)S(1)}, bf16[64,1024]{1,0:T(8,128)(2,1)S(1)}, u32[]{:S(2)}, u32[]{:S(2)}) collective-permute-start(bf16[64,1024]{1,0:T(8,128)(2,1)S(1)} %add_convert_fusion), channel_id=1, source_target_pairs={{0,192},{16,208},{32,224},{48,240},{64,128},{80,144},{96,160},{112... | collective-permute-start | bytes 393224 | tf_op jit(solution)/shard_map/ppermute | solution.py:221
  36.6 9.8 %collective-permute-start.6 = (bf16[64,1024]{1,0:T(8,128)(2,1)S(1)}, bf16[64,1024]{1,0:T(8,128)(2,1)S(1)}, u32[]{:S(2)}, u32[]{:S(2)}) collective-permute-start(bf16[64,1024]{1,0:T(8,128)(2,1)S(1)} %add_convert_fusion.2), channel_id=1, source_target_pairs={{0,64},{16,80},{32,96},{48,112},{64,0},{80,16},{96,32},{112,48},{1... | collective-permute-start | bytes 393224 | tf_op jit(solution)/shard_map/ppermute | solution.py:221
  41.6 7.9 %collective-permute-start.17 = (bf16[64,1024]{1,0:T(8,128)(2,1)S(1)}, bf16[64,1024]{1,0:T(8,128)(2,1)S(1)}, u32[]{:S(2)}, u32[]{:S(2)}) collective-permute-start(bf16[64,1024]{1,0:T(8,128)(2,1)S(1)} %get-tuple-element.42.refs_0_), channel_id=1, source_target_pairs={{0,32},{16,48},{32,0},{48,16},{64,96},{80,112},{96,64},{112,80},{1... | collective-permute-start | bytes 393224 | tf_op jit(solution)/shard_map/ppermute | solution.py:221
  43.2 8.9 %collective-permute-start.16 = (bf16[64,1024]{1,0:T(8,128)(2,1)S(1)}, bf16[64,1024]{1,0:T(8,128)(2,1)S(1)}, u32[]{:S(2)}, u32[]{:S(2)}) collective-permute-start(bf16[64,1024]{1,0:T(8,128)(2,1)S(1)} %get-tuple-element.42.refs_0_), channel_id=1, source_target_pairs={{0,16},{16,32},{32,48},{48,0},{64,80},{80,96},{96,112},{112,64},{1... | collective-permute-start | bytes 393224 | tf_op jit(solution)/shard_map/ppermute | solution.py:221
  45.9 6.2 %collective-permute-start.15 = (bf16[64,1024]{1,0:T(8,128)(2,1)S(1)}, bf16[64,1024]{1,0:T(8,128)(2,1)S(1)}, u32[]{:S(2)}, u32[]{:S(2)}) collective-permute-start(bf16[64,1024]{1,0:T(8,128)(2,1)S(1)} %get-tuple-element.42.refs_0_), channel_id=1, source_target_pairs={{0,48},{16,0},{32,16},{48,32},{64,112},{80,64},{96,80},{112,96},{1... | collective-permute-start | bytes 393224 | tf_op jit(solution)/shard_map/ppermute | solution.py:221
  46.6 7.3 %collective-permute-start.9 = (bf16[64,1024]{1,0:T(8,128)(2,1)S(1)}, bf16[64,1024]{1,0:T(8,128)(2,1)S(1)}, u32[]{:S(2)}, u32[]{:S(2)}) collective-permute-start(bf16[64,1024]{1,0:T(8,128)(2,1)S(1)} %get-tuple-element.40.refs_0_), channel_id=1, source_target_pairs={{0,32},{16,48},{32,0},{48,16},{64,96},{80,112},{96,64},{112,80},{1... | collective-permute-start | bytes 393224 | tf_op jit(solution)/shard_map/ppermute | solution.py:221
  48.8 6.2 %collective-permute-start.8 = (bf16[64,1024]{1,0:T(8,128)(2,1)S(1)}, bf16[64,1024]{1,0:T(8,128)(2,1)S(1)}, u32[]{:S(2)}, u32[]{:S(2)}) collective-permute-start(bf16[64,1024]{1,0:T(8,128)(2,1)S(1)} %get-tuple-element.40.refs_0_), channel_id=1, source_target_pairs={{0,16},{16,32},{32,48},{48,0},{64,80},{80,96},{96,112},{112,64},{1... | collective-permute-start | bytes 393224 | tf_op jit(solution)/shard_map/ppermute | solution.py:221
  49.5 5.5 %collective-permute-start.7 = (bf16[64,1024]{1,0:T(8,128)(2,1)S(1)}, bf16[64,1024]{1,0:T(8,128)(2,1)S(1)}, u32[]{:S(2)}, u32[]{:S(2)}) collective-permute-start(bf16[64,1024]{1,0:T(8,128)(2,1)S(1)} %get-tuple-element.40.refs_0_), channel_id=1, source_target_pairs={{0,48},{16,0},{32,16},{48,32},{64,112},{80,64},{96,80},{112,96},{1... | collective-permute-start | bytes 393224 | tf_op jit(solution)/shard_map/ppermute | solution.py:221

commit v5 on v4

--- a/solution.py
+++ b/solution.py
@@ -244,7 +244,7 @@
     others = others_copied(ids, moments[0], inner)
     grads, news = [], []
     for c in range(CHUNKS):
-        order = (1, 3) if c % 2 == 0 else (3, 1)
+        order = (1, 3)
         part = parts[c]
         part = (part.astype(f32) + send(part, z_swap(order[0])).astype(f32)).astype(bf16)
         if c == CHUNKS - 1:

time: 56.7 us -> 57.9 us (1.021)
  waiting for transfers between devices: 4.93 us -> 10.9 us
  starting transfers between devices: 40 us -> 35.3 us
    ppermute x18, waiting for transfers between devices: 4.93 us -> 10.9 us  [send(): return lax.ppermute(x, 'replica', perm)]
    ppermute x18, starting transfers between devices: 40 us -> 35.3 us  [send(): return lax.ppermute(x, 'replica', perm)]
  transfers between devices with their start and end apart: 18 -> 18, of which waited for: 5 -> 7; matrix products, arithmetic and copies ran while one was open for 2% -> 2% of each run, Pallas kernels for 13% -> 13%
where the time goes in v5:
time: 57.9 us; the launch traced here: 57.3 us
  starting transfers between devices  35.3 us (61%)
  waiting for transfers between devices  10.9 us (19%)
  Pallas kernels  8.4 us (15%)
  between operations  1.41 us (2%)
  other arithmetic  1.29 us (2%)
    ppermute x18, starting transfers between devices, send(): return lax.ppermute(x, 'replica', perm)  35.3 us
    ppermute x18, waiting for transfers between devices, send(): return lax.ppermute(x, 'replica', perm)  10.9 us
    pallas_call x2, Pallas kernels, rounded_blocks(): pl.pallas_call(functools.partial(round_kernel, chunk, share), out_shape=[...  3.51 us
    pallas_call x1, Pallas kernels, others_copied(): pl.pallas_call(copy_kernel, out_shape=jax.ShapeDtypeStruct(inner.shape, i...  2.81 us
    pallas_call x2, Pallas kernels, blended(): pl.pallas_call(functools.partial(blend_kernel, chunk, share), out_shape=[...  2.08 us
  transfers between devices with their start and end apart: 18, of which 7 were waited for; matrix products, arithmetic and copies ran while one was open for 2% of the time, Pallas kernels for 13%

profile of v5, /device:TPU:2, one launch (start us, length us, event | category | flops | bytes accessed | tf_op | source)
XLA Modules:
  0.0 57.3 jit_solution(8404983484574851972)
XLA Ops:
  0.6 3.4 %collective-permute-start = (f32[64,512]{1,0:T(8,128)}, f32[64,512]{1,0:T(8,128)S(1)}, u32[]{:S(2)}, u32[]{:S(2)}) collective-permute-start(f32[64,512]{1,0:T(8,128)} %param.7), channel_id=1, source_target_pairs={{0,64},{16,80},{32,96},{48,112},{64,0},{80,16},{96,32},{112,48},{1... | collective-permute-start | bytes 393224 | tf_op jit(solution)/shard_map/ppermute | solution.py:221
  4.6 1.8 %round0.1 = (bf16[64,1024]{1,0:T(8,128)(2,1)S(1)}, bf16[64,1024]{1,0:T(8,128)(2,1)S(1)}, bf16[64,1024]{1,0:T(8,128)(2,1)S(1)}, bf16[64,1024]{1,0:T(8,128)(2,1)S(...) custom-call(s32[1]{0:T(128)S(6)} %copy.14.ids.after_ref, s32[1]{0:T(128)S(6)} %copy.14.ids.after_ref, ...), custom_call_target="tpu_custom_call" | custom-call | flops 3145728 | bytes 2621440 | tf_op jit(solution)/shard_map/round0/pallas_call | solution.py:86
  6.4 1.7 %collective-permute-start.10 = (bf16[64,1024]{1,0:T(8,128)(2,1)S(1)}, bf16[64,1024]{1,0:T(8,128)(2,1)S(1)}, u32[]{:S(2)}, u32[]{:S(2)}) collective-permute-start(bf16[64,1024]{1,0:T(8,128)(2,1)S(1)} %get-tuple-element.31), channel_id=1, source_target_pairs={{0,16},{16,32},{32,48},{48,0},{64,80},{80,96},{96,112},{112,64},{1... | collective-permute-start | bytes 393224 | tf_op jit(solution)/shard_map/ppermute | solution.py:221
  8.1 2.9 %collective-permute-start.11 = (bf16[64,1024]{1,0:T(8,128)(2,1)S(1)}, bf16[64,1024]{1,0:T(8,128)(2,1)S(1)}, u32[]{:S(2)}, u32[]{:S(2)}) collective-permute-start(bf16[64,1024]{1,0:T(8,128)(2,1)S(1)} %get-tuple-element.32), channel_id=1, source_target_pairs={{0,32},{16,48},{32,0},{48,16},{64,96},{80,112},{96,64},{112,80},{1... | collective-permute-start | bytes 393224 | tf_op jit(solution)/shard_map/ppermute | solution.py:221
  11.0 1.3 %collective-permute-start.12 = (bf16[64,1024]{1,0:T(8,128)(2,1)S(1)}, bf16[64,1024]{1,0:T(8,128)(2,1)S(1)}, u32[]{:S(2)}, u32[]{:S(2)}) collective-permute-start(bf16[64,1024]{1,0:T(8,128)(2,1)S(1)} %get-tuple-element.33), channel_id=1, source_target_pairs={{0,48},{16,0},{32,16},{48,32},{64,112},{80,64},{96,80},{112,96},{1... | collective-permute-start | bytes 393224 | tf_op jit(solution)/shard_map/ppermute | solution.py:221
  12.4 4.6 %collective-permute-start.5 = (f32[64,1024]{1,0:T(8,128)S(1)}, f32[64,1024]{1,0:T(8,128)S(1)}, u32[]{:S(2)}, u32[]{:S(2)}) collective-permute-start(f32[64,1024]{1,0:T(8,128)S(1)} %pad_maximum_fusion.after_ref), channel_id=1, source_target_pairs={{0,192},{16,208},{32,224},{48,240},{64,128},{80,144},{96,160},{112... | collective-permute-start | bytes 786440 | tf_op jit(solution)/shard_map/ppermute | solution.py:221
  16.9 1.8 %round1.1 = (bf16[64,1024]{1,0:T(8,128)(2,1)S(1)}, bf16[64,1024]{1,0:T(8,128)(2,1)S(1)}, bf16[64,1024]{1,0:T(8,128)(2,1)S(1)}, bf16[64,1024]{1,0:T(8,128)(2,1)S(...) custom-call(s32[1]{0:T(128)S(6)} %copy.14.ids.after_ref, f32[64,1024]{1,0:T(8,128)S(1)} %pad_maximum_fusion.after_ref, ...), custom_call_target="tpu_custom_call" | custom-call | flops 3145728 | bytes 2621440 | tf_op jit(solution)/shard_map/round1/pallas_call | solution.py:86
  18.7 0.8 %collective-permute-start.1 = (bf16[64,1024]{1,0:T(8,128)(2,1)S(1)}, bf16[64,1024]{1,0:T(8,128)(2,1)S(1)}, u32[]{:S(2)}, u32[]{:S(2)}) collective-permute-start(bf16[64,1024]{1,0:T(8,128)(2,1)S(1)} %get-tuple-element.24), channel_id=1, source_target_pairs={{0,16},{16,32},{32,48},{48,0},{64,80},{80,96},{96,112},{112,64},{1... | collective-permute-start | bytes 393224 | tf_op jit(solution)/shard_map/ppermute | solution.py:221
  19.5 1.4 %collective-permute-start.2 = (bf16[64,1024]{1,0:T(8,128)(2,1)S(1)}, bf16[64,1024]{1,0:T(8,128)(2,1)S(1)}, u32[]{:S(2)}, u32[]{:S(2)}) collective-permute-start(bf16[64,1024]{1,0:T(8,128)(2,1)S(1)} %get-tuple-element.25), channel_id=1, source_target_pairs={{0,32},{16,48},{32,0},{48,16},{64,96},{80,112},{96,64},{112,80},{1... | collective-permute-start | bytes 393224 | tf_op jit(solution)/shard_map/ppermute | solution.py:221
  20.8 1.4 %collective-permute-start.3 = (bf16[64,1024]{1,0:T(8,128)(2,1)S(1)}, bf16[64,1024]{1,0:T(8,128)(2,1)S(1)}, u32[]{:S(2)}, u32[]{:S(2)}) collective-permute-start(bf16[64,1024]{1,0:T(8,128)(2,1)S(1)} %get-tuple-element.26), channel_id=1, source_target_pairs={{0,48},{16,0},{32,16},{48,32},{64,112},{80,64},{96,80},{112,96},{1... | collective-permute-start | bytes 393224 | tf_op jit(solution)/shard_map/ppermute | solution.py:221
  22.3 3.3 %collective-permute-start.13 = (bf16[64,1024]{1,0:T(8,128)(2,1)S(1)}, bf16[64,1024]{1,0:T(8,128)(2,1)S(1)}, u32[]{:S(2)}, u32[]{:S(2)}) collective-permute-start(bf16[64,1024]{1,0:T(8,128)(2,1)S(1)} %add_convert_fusion.1), channel_id=1, source_target_pairs={{0,64},{16,80},{32,96},{48,112},{64,0},{80,16},{96,32},{112,48},{1... | collective-permute-start | bytes 393224 | tf_op jit(solution)/shard_map/ppermute | solution.py:221
  25.6 1.2 %collective-permute-done.1 = bf16[64,1024]{1,0:T(8,128)(2,1)S(1)} collective-permute-done((bf16[64,1024]{1,0:T(8,128)(2,1)S(1)}, bf16[64,1024]{1,0:T(8,128)(2,1)S(1)}, u32[]{:S(2)}, u32[]{:S(2)}) %collective-permute-start.1) | collective-permute-done | bytes 131104 | tf_op jit(solution)/shard_map/ppermute | solution.py:221
  27.3 2.4 %collective-permute-start.4 = (bf16[64,1024]{1,0:T(8,128)(2,1)S(1)}, bf16[64,1024]{1,0:T(8,128)(2,1)S(1)}, u32[]{:S(2)}, u32[]{:S(2)}) collective-permute-start(bf16[64,1024]{1,0:T(8,128)(2,1)S(1)} %add_convert_fusion.3), channel_id=1, source_target_pairs={{0,64},{16,80},{32,96},{48,112},{64,0},{80,16},{96,32},{112,48},{1... | collective-permute-start | bytes 393224 | tf_op jit(solution)/shard_map/ppermute | solution.py:221
  29.8 5.2 %collective-permute-start.14 = (bf16[64,1024]{1,0:T(8,128)(2,1)S(1)}, bf16[64,1024]{1,0:T(8,128)(2,1)S(1)}, u32[]{:S(2)}, u32[]{:S(2)}) collective-permute-start(bf16[64,1024]{1,0:T(8,128)(2,1)S(1)} %add_convert_fusion), channel_id=1, source_target_pairs={{0,192},{16,208},{32,224},{48,240},{64,128},{80,144},{96,160},{112... | collective-permute-start | bytes 393224 | tf_op jit(solution)/shard_map/ppermute | solution.py:221
  35.0 2.8 %others.1.refs_4_ = bf16[1,4,64,8192]{3,2,1,0:T(8,128)(2,1)} custom-call(s32[1]{0:T(128)S(6)} %copy.14.ids.after_ref, f32[64,512]{1,0:T(8,128)S(1)} %get-tuple-element.48.after_ref, bf16[1,4,64,8192]{3,2,1,0:T(8,128)(2,1)} %inner_hbm.5), custom_call_target="tpu_custom_call" | custom-call | bytes 6291456 | tf_op jit(solution)/shard_map/others/pallas_call | solution.py:134
  38.0 4.6 %collective-permute-done.14 = bf16[64,1024]{1,0:T(8,128)(2,1)S(1)} collective-permute-done((bf16[64,1024]{1,0:T(8,128)(2,1)S(1)}, bf16[64,1024]{1,0:T(8,128)(2,1)S(1)}, u32[]{:S(2)}, u32[]{:S(2)}) %collective-permute-start.14) | collective-permute-done | bytes 131104 | tf_op jit(solution)/shard_map/ppermute | solution.py:221
  43.0 3.2 %collective-permute-start.15 = (bf16[64,1024]{1,0:T(8,128)(2,1)S(1)}, bf16[64,1024]{1,0:T(8,128)(2,1)S(1)}, u32[]{:S(2)}, u32[]{:S(2)}) collective-permute-start(bf16[64,1024]{1,0:T(8,128)(2,1)S(1)} %get-tuple-element.42.refs_0_), channel_id=1, source_target_pairs={{0,48},{16,0},{32,16},{48,32},{64,112},{80,64},{96,80},{112,96},{1... | collective-permute-start | bytes 393224 | tf_op jit(solution)/shard_map/ppermute | solution.py:221
  46.4 2.3 %collective-permute-start.9 = (bf16[64,1024]{1,0:T(8,128)(2,1)S(1)}, bf16[64,1024]{1,0:T(8,128)(2,1)S(1)}, u32[]{:S(2)}, u32[]{:S(2)}) collective-permute-start(bf16[64,1024]{1,0:T(8,128)(2,1)S(1)} %get-tuple-element.40.refs_0_), channel_id=1, source_target_pairs={{0,32},{16,48},{32,0},{48,16},{64,96},{80,112},{96,64},{112,80},{1... | collective-permute-start | bytes 393224 | tf_op jit(solution)/shard_map/ppermute | solution.py:221
  48.7 2.0 %collective-permute-done.17.refs_3_ = bf16[64,1024]{1,0:T(8,128)(2,1)S(1)} collective-permute-done((bf16[64,1024]{1,0:T(8,128)(2,1)S(1)}, bf16[64,1024]{1,0:T(8,128)(2,1)S(1)}, u32[]{:S(2)}, u32[]{:S(2)}) %collective-permute-start.17) | collective-permute-done | bytes 131104 | tf_op jit(solution)/shard_map/ppermute | solution.py:221
  50.7 1.2 %collective-permute-start.7 = (bf16[64,1024]{1,0:T(8,128)(2,1)S(1)}, bf16[64,1024]{1,0:T(8,128)(2,1)S(1)}, u32[]{:S(2)}, u32[]{:S(2)}) collective-permute-start(bf16[64,1024]{1,0:T(8,128)(2,1)S(1)} %get-tuple-element.40.refs_0_), channel_id=1, source_target_pairs={{0,48},{16,0},{32,16},{48,32},{64,112},{80,64},{96,80},{112,96},{1... | collective-permute-start | bytes 393224 | tf_op jit(solution)/shard_map/ppermute | solution.py:221
  51.9 1.1 %collective-permute-done.16.refs_2_ = bf16[64,1024]{1,0:T(8,128)(2,1)S(1)} collective-permute-done((bf16[64,1024]{1,0:T(8,128)(2,1)S(1)}, bf16[64,1024]{1,0:T(8,128)(2,1)S(1)}, u32[]{:S(2)}, u32[]{:S(2)}) %collective-permute-start.16) | collective-permute-done | bytes 131104 | tf_op jit(solution)/shard_map/ppermute | solution.py:221
  53.1 1.0 %blend0.1 = (bf16[64,8192]{1,0:T(8,128)(2,1)}, bf16[1,4,64,8192]{3,2,1,0:T(8,128)(2,1)}) custom-call(s32[1]{0:T(128)S(6)} %copy.14.ids.after_ref, bf16[64,4096]{1,0:T(8,128)(2,1)S(1)} %get-tuple-element.28.chosen, bf16[64,1024]{1,0:T(8,128)(2,1)S(1)} %get-tuple-element.42.refs_0_, ...), custom_call_target="tpu_custom_call", output_to_operand_aliasing={{1}: (6, {})} | custom-call | flops 1048576 | bytes 2097152 | tf_op jit(solution)/shard_map/blend0/pallas_call | solution.py:192
  55.1 1.1 %collective-permute-done.8.refs_2_ = bf16[64,1024]{1,0:T(8,128)(2,1)S(1)} collective-permute-done((bf16[64,1024]{1,0:T(8,128)(2,1)S(1)}, bf16[64,1024]{1,0:T(8,128)(2,1)S(1)}, u32[]{:S(2)}, u32[]{:S(2)}) %collective-permute-start.8) | collective-permute-done | bytes 131104 | tf_op jit(solution)/shard_map/ppermute | solution.py:221
  56.3 1.0 %blend1.1 = (bf16[64,8192]{1,0:T(8,128)(2,1)}, bf16[1,4,64,8192]{3,2,1,0:T(8,128)(2,1)}) custom-call(s32[1]{0:T(128)S(6)} %copy.14.ids.after_ref, bf16[64,4096]{1,0:T(8,128)(2,1)S(1)} %get-tuple-element.21.chosen, bf16[64,1024]{1,0:T(8,128)(2,1)S(1)} %get-tuple-element.40.refs_0_, ...), custom_call_target="tpu_custom_call", output_to_operand_aliasing={{0}: (6, {}), {1}: (7, {})} | custom-call | flops 1048576 | bytes 2097152 | tf_op jit(solution)/shard_map/blend1/pallas_call | solution.py:192
  (29 shorter events, 2.3 us)
Async XLA Ops:
  0.6 11.7 %copy-start = (f32[64,512]{1,0:T(8,128)S(1)}, f32[64,512]{1,0:T(8,128)}, u32[]{:S(2)}) copy-start(f32[64,512]{1,0:T(8,128)} %param.7) | copy-start | bytes 393220
  0.6 11.7 %collective-permute-start = (f32[64,512]{1,0:T(8,128)}, f32[64,512]{1,0:T(8,128)S(1)}, u32[]{:S(2)}, u32[]{:S(2)}) collective-permute-start(f32[64,512]{1,0:T(8,128)} %param.7), channel_id=1, source_target_pairs={{0,64},{16,80},{32,96},{48,112},{64,0},{80,16},{96,32},{112,48},{1... | collective-permute-start | bytes 393224 | tf_op jit(solution)/shard_map/ppermute | solution.py:221
  6.4 13.1 %collective-permute-start.10 = (bf16[64,1024]{1,0:T(8,128)(2,1)S(1)}, bf16[64,1024]{1,0:T(8,128)(2,1)S(1)}, u32[]{:S(2)}, u32[]{:S(2)}) collective-permute-start(bf16[64,1024]{1,0:T(8,128)(2,1)S(1)} %get-tuple-element.31), channel_id=1, source_target_pairs={{0,16},{16,32},{32,48},{48,0},{64,80},{80,96},{96,112},{112,64},{1... | collective-permute-start | bytes 393224 | tf_op jit(solution)/shard_map/ppermute | solution.py:221
  8.1 12.8 %collective-permute-start.11 = (bf16[64,1024]{1,0:T(8,128)(2,1)S(1)}, bf16[64,1024]{1,0:T(8,128)(2,1)S(1)}, u32[]{:S(2)}, u32[]{:S(2)}) collective-permute-start(bf16[64,1024]{1,0:T(8,128)(2,1)S(1)} %get-tuple-element.32), channel_id=1, source_target_pairs={{0,32},{16,48},{32,0},{48,16},{64,96},{80,112},{96,64},{112,80},{1... | collective-permute-start | bytes 393224 | tf_op jit(solution)/shard_map/ppermute | solution.py:221
  11.0 11.3 %collective-permute-start.12 = (bf16[64,1024]{1,0:T(8,128)(2,1)S(1)}, bf16[64,1024]{1,0:T(8,128)(2,1)S(1)}, u32[]{:S(2)}, u32[]{:S(2)}) collective-permute-start(bf16[64,1024]{1,0:T(8,128)(2,1)S(1)} %get-tuple-element.33), channel_id=1, source_target_pairs={{0,48},{16,0},{32,16},{48,32},{64,112},{80,64},{96,80},{112,96},{1... | collective-permute-start | bytes 393224 | tf_op jit(solution)/shard_map/ppermute | solution.py:221
  12.4 22.6 %collective-permute-start.5 = (f32[64,1024]{1,0:T(8,128)S(1)}, f32[64,1024]{1,0:T(8,128)S(1)}, u32[]{:S(2)}, u32[]{:S(2)}) collective-permute-start(f32[64,1024]{1,0:T(8,128)S(1)} %pad_maximum_fusion.after_ref), channel_id=1, source_target_pairs={{0,192},{16,208},{32,224},{48,240},{64,128},{80,144},{96,160},{112... | collective-permute-start | bytes 786440 | tf_op jit(solution)/shard_map/ppermute | solution.py:221
  18.7 8.1 %collective-permute-start.1 = (bf16[64,1024]{1,0:T(8,128)(2,1)S(1)}, bf16[64,1024]{1,0:T(8,128)(2,1)S(1)}, u32[]{:S(2)}, u32[]{:S(2)}) collective-permute-start(bf16[64,1024]{1,0:T(8,128)(2,1)S(1)} %get-tuple-element.24), channel_id=1, source_target_pairs={{0,16},{16,32},{32,48},{48,0},{64,80},{80,96},{96,112},{112,64},{1... | collective-permute-start | bytes 393224 | tf_op jit(solution)/shard_map/ppermute | solution.py:221
  19.5 7.4 %collective-permute-start.2 = (bf16[64,1024]{1,0:T(8,128)(2,1)S(1)}, bf16[64,1024]{1,0:T(8,128)(2,1)S(1)}, u32[]{:S(2)}, u32[]{:S(2)}) collective-permute-start(bf16[64,1024]{1,0:T(8,128)(2,1)S(1)} %get-tuple-element.25), channel_id=1, source_target_pairs={{0,32},{16,48},{32,0},{48,16},{64,96},{80,112},{96,64},{112,80},{1... | collective-permute-start | bytes 393224 | tf_op jit(solution)/shard_map/ppermute | solution.py:221
  20.8 6.4 %collective-permute-start.3 = (bf16[64,1024]{1,0:T(8,128)(2,1)S(1)}, bf16[64,1024]{1,0:T(8,128)(2,1)S(1)}, u32[]{:S(2)}, u32[]{:S(2)}) collective-permute-start(bf16[64,1024]{1,0:T(8,128)(2,1)S(1)} %get-tuple-element.26), channel_id=1, source_target_pairs={{0,48},{16,0},{32,16},{48,32},{64,112},{80,64},{96,80},{112,96},{1... | collective-permute-start | bytes 393224 | tf_op jit(solution)/shard_map/ppermute | solution.py:221
  22.3 7.4 %collective-permute-start.13 = (bf16[64,1024]{1,0:T(8,128)(2,1)S(1)}, bf16[64,1024]{1,0:T(8,128)(2,1)S(1)}, u32[]{:S(2)}, u32[]{:S(2)}) collective-permute-start(bf16[64,1024]{1,0:T(8,128)(2,1)S(1)} %add_convert_fusion.1), channel_id=1, source_target_pairs={{0,64},{16,80},{32,96},{48,112},{64,0},{80,16},{96,32},{112,48},{1... | collective-permute-start | bytes 393224 | tf_op jit(solution)/shard_map/ppermute | solution.py:221
  27.3 10.5 %collective-permute-start.4 = (bf16[64,1024]{1,0:T(8,128)(2,1)S(1)}, bf16[64,1024]{1,0:T(8,128)(2,1)S(1)}, u32[]{:S(2)}, u32[]{:S(2)}) collective-permute-start(bf16[64,1024]{1,0:T(8,128)(2,1)S(1)} %add_convert_fusion.3), channel_id=1, source_target_pairs={{0,64},{16,80},{32,96},{48,112},{64,0},{80,16},{96,32},{112,48},{1... | collective-permute-start | bytes 393224 | tf_op jit(solution)/shard_map/ppermute | solution.py:221
  29.8 12.8 %collective-permute-start.14 = (bf16[64,1024]{1,0:T(8,128)(2,1)S(1)}, bf16[64,1024]{1,0:T(8,128)(2,1)S(1)}, u32[]{:S(2)}, u32[]{:S(2)}) collective-permute-start(bf16[64,1024]{1,0:T(8,128)(2,1)S(1)} %add_convert_fusion), channel_id=1, source_target_pairs={{0,192},{16,208},{32,224},{48,240},{64,128},{80,144},{96,160},{112... | collective-permute-start | bytes 393224 | tf_op jit(solution)/shard_map/ppermute | solution.py:221
  37.9 8.3 %collective-permute-start.6 = (bf16[64,1024]{1,0:T(8,128)(2,1)S(1)}, bf16[64,1024]{1,0:T(8,128)(2,1)S(1)}, u32[]{:S(2)}, u32[]{:S(2)}) collective-permute-start(bf16[64,1024]{1,0:T(8,128)(2,1)S(1)} %add_convert_fusion.2), channel_id=1, source_target_pairs={{0,192},{16,208},{32,224},{48,240},{64,128},{80,144},{96,160},{112... | collective-permute-start | bytes 393224 | tf_op jit(solution)/shard_map/ppermute | solution.py:221
  42.8 7.9 %collective-permute-start.17 = (bf16[64,1024]{1,0:T(8,128)(2,1)S(1)}, bf16[64,1024]{1,0:T(8,128)(2,1)S(1)}, u32[]{:S(2)}, u32[]{:S(2)}) collective-permute-start(bf16[64,1024]{1,0:T(8,128)(2,1)S(1)} %get-tuple-element.42.refs_0_), channel_id=1, source_target_pairs={{0,32},{16,48},{32,0},{48,16},{64,96},{80,112},{96,64},{112,80},{1... | collective-permute-start | bytes 393224 | tf_op jit(solution)/shard_map/ppermute | solution.py:221
  42.9 10.2 %collective-permute-start.16 = (bf16[64,1024]{1,0:T(8,128)(2,1)S(1)}, bf16[64,1024]{1,0:T(8,128)(2,1)S(1)}, u32[]{:S(2)}, u32[]{:S(2)}) collective-permute-start(bf16[64,1024]{1,0:T(8,128)(2,1)S(1)} %get-tuple-element.42.refs_0_), channel_id=1, source_target_pairs={{0,16},{16,32},{32,48},{48,0},{64,80},{80,96},{96,112},{112,64},{1... | collective-permute-start | bytes 393224 | tf_op jit(solution)/shard_map/ppermute | solution.py:221
  43.0 10.1 %collective-permute-start.15 = (bf16[64,1024]{1,0:T(8,128)(2,1)S(1)}, bf16[64,1024]{1,0:T(8,128)(2,1)S(1)}, u32[]{:S(2)}, u32[]{:S(2)}) collective-permute-start(bf16[64,1024]{1,0:T(8,128)(2,1)S(1)} %get-tuple-element.42.refs_0_), channel_id=1, source_target_pairs={{0,48},{16,0},{32,16},{48,32},{64,112},{80,64},{96,80},{112,96},{1... | collective-permute-start | bytes 393224 | tf_op jit(solution)/shard_map/ppermute | solution.py:221
  46.4 8.8 %collective-permute-start.9 = (bf16[64,1024]{1,0:T(8,128)(2,1)S(1)}, bf16[64,1024]{1,0:T(8,128)(2,1)S(1)}, u32[]{:S(2)}, u32[]{:S(2)}) collective-permute-start(bf16[64,1024]{1,0:T(8,128)(2,1)S(1)} %get-tuple-element.40.refs_0_), channel_id=1, source_target_pairs={{0,32},{16,48},{32,0},{48,16},{64,96},{80,112},{96,64},{112,80},{1... | collective-permute-start | bytes 393224 | tf_op jit(solution)/shard_map/ppermute | solution.py:221
  48.7 7.6 %collective-permute-start.8 = (bf16[64,1024]{1,0:T(8,128)(2,1)S(1)}, bf16[64,1024]{1,0:T(8,128)(2,1)S(1)}, u32[]{:S(2)}, u32[]{:S(2)}) collective-permute-start(bf16[64,1024]{1,0:T(8,128)(2,1)S(1)} %get-tuple-element.40.refs_0_), channel_id=1, source_target_pairs={{0,16},{16,32},{32,48},{48,0},{64,80},{80,96},{96,112},{112,64},{1... | collective-permute-start | bytes 393224 | tf_op jit(solution)/shard_map/ppermute | solution.py:221
  50.7 5.5 %collective-permute-start.7 = (bf16[64,1024]{1,0:T(8,128)(2,1)S(1)}, bf16[64,1024]{1,0:T(8,128)(2,1)S(1)}, u32[]{:S(2)}, u32[]{:S(2)}) collective-permute-start(bf16[64,1024]{1,0:T(8,128)(2,1)S(1)} %get-tuple-element.40.refs_0_), channel_id=1, source_target_pairs={{0,48},{16,0},{32,16},{48,32},{64,112},{80,64},{96,80},{112,96},{1... | collective-permute-start | bytes 393224 | tf_op jit(solution)/shard_map/ppermute | solution.py:221
